TPU v7x, 128 devices: a whole 4x4x4 slice. The times are simulated.
128 devices in a mesh: stream: 32 (over x, z, core), span: 4 (over y).
Axes of the slice: x: 4, y: 4, z: 4, core: 2. Of those that a mesh axis runs over, the one named last changes fastest.
Arguments:
- basis: float32 [4, 64, 65536], P(None, None, ('stream', 'span')), may hold values from -5.6 to 5.6
- interface_row_owner: int32 [131072, 1], P(('stream', 'span')), may hold values from 0 to 127; in each aligned block of 1024 rows (0 to 1023, 1024 to 2047, ...) at most 16 rows name the same one
- interface_local_row: int32 [131072], P(('stream', 'span')), may hold values from 0 to 511
- interface_slot_weight: float32 [131072], P(('stream', 'span')), may hold values from 0.25 to 1
- local_inverse: bfloat16 [64, 64, 131072], P(None, None, ('stream', 'span')), may hold values from -0.75 to 1.55
- prim_index: int32 [4096], P(('stream', 'span')), may hold values from 0 to 1023
- prim_vector: float32 [64, 4096], P(None, ('stream', 'span')), may hold values from -4 to 4
- coarse_inverse: float32 [1024, 1024], P('stream'), may hold values from -0.1875 to 0.1875
- interface_shifted_diagonal: float32 [64, 131072], P(None, ('stream', 'span')), may hold values from 2 to 4
- coupling_index: int32 [2, 65536], P(None, ('stream', 'span')), may hold values from 0 to 1023
- coupling_blocks: bfloat16 [2, 64, 64, 65536], P(None, None, None, ('stream', 'span')), may hold values from -0.75 to 0.75
- interior_inverse: bfloat16 [64, 64, 65536], P(None, None, ('stream', 'span')), may hold values from -0.75 to 1.55
Outputs:
- direction: float32 [64, 65536], P(None, ('stream', 'span'))
- coeffs: float32 [5], replicated
Inputs may be any that keep to these rules, and one draw needn't show every extreme that they name: `interface_row_owner`: in the slots of one subdomain (aligned blocks of 1024 slots) no owner is named more than 16 times, a bound that some block reaches.
All inputs are finite; a program needn't handle non-finite values.
Results may differ from a plain program's by a relative error of at most 0.0003.
Values sent between devices are 32-bit elements; how exact they have to be, the bound alone decides.
No kernel may reach another device: no remote copies, remote signals or barrier semaphores. Data moves between devices by JAX's collectives and lax.ppermute only.
A program may use at most 64 MiB of HBM per device.

v0:
```python
import functools
import math

import jax
import jax.numpy as jnp
from jax import lax
from jax.experimental import pallas as pl
from jax.experimental.pallas import tpu as pltpu
from jax.sharding import PartitionSpec as P

HIGH = lax.Precision.HIGHEST
F32 = jnp.float32
BF16 = jnp.bfloat16
LANES = 128
PAIRS = 8


def split(x):
    high = x.astype(BF16)
    return high, (x - high.astype(F32)).astype(BF16)


def mm(a, b):
    return jnp.dot(a, b, preferred_element_type=F32)


def mm_nt(a, b, precision=None):
    return lax.dot_general(a, b, (((1,), (1,)), ((), ())), precision=precision, preferred_element_type=F32)


def one_hot(mask):
    return jnp.where(mask, 1.0, 0.0).astype(BF16)


def message_rows(k, count):
    return pl.ds(k, count, stride=PAIRS)


def call(kernel, out_shape, *args, vmem=16, **kw):
    return pl.pallas_call(
        kernel,
        out_shape=out_shape,
        compiler_params=pltpu.CompilerParams(vmem_limit_bytes=vmem * 1024 * 1024),
        **kw,
    )(*args)


def plan_kernel(owner_ref, row_ref, request_ref, rank_ref):
    slots = owner_ref.shape[1]
    devices = request_ref.shape[0]
    owner = owner_ref[...]
    row = row_ref[...]
    named = one_hot(lax.broadcasted_iota(jnp.int32, (devices, slots), 0) == owner)
    before = lax.broadcasted_iota(jnp.int32, (LANES, LANES), 0) < lax.broadcasted_iota(
        jnp.int32, (LANES, LANES), 1
    )
    counter = jnp.concatenate([one_hot(before), jnp.ones((LANES, LANES), BF16)], axis=1)
    carry = jnp.zeros((devices, LANES), F32)
    ranks = []
    for block in range(slots // LANES):
        part = named[:, block * LANES : (block + 1) * LANES]
        counts = mm(part, counter)
        ranks.append(jnp.sum((counts[:, :LANES] + carry) * part.astype(F32), axis=0, keepdims=True))
        carry = carry + counts[:, LANES:]
    rank = jnp.concatenate(ranks, axis=1).astype(jnp.int32)
    rank_ref[...] = rank
    at_rank = lax.broadcasted_iota(jnp.int32, (LANES, slots), 0) == rank
    tens = jnp.where(at_rank, (row >> 4).astype(F32), 0.0).astype(BF16)
    units = jnp.where(at_rank, (row & 15).astype(F32), 0.0).astype(BF16)
    request_ref[...] = (16.0 * mm_nt(named, tens) + mm_nt(named, units)).astype(jnp.int32)


def slots_from_messages(message_ref, owner, rank):
    slots = owner.shape[1]
    devices = message_ref.shape[0] // PAIRS
    width = LANES // 2
    sides = []
    for k in range(PAIRS):
        high, low = split(message_ref[message_rows(k, devices), :].T)
        sides.append(jnp.concatenate([high, low], axis=1))
    chunk = 256
    pieces = []
    for c in range(slots // chunk):
        lanes = slice(c * chunk, (c + 1) * chunk)
        named = one_hot(lax.broadcasted_iota(jnp.int32, (devices, chunk), 0) == owner[:, lanes])
        named = jnp.concatenate([named, named], axis=0)
        place = jnp.broadcast_to(rank[:, lanes], (width, chunk))
        total = jnp.zeros((width, chunk), F32)
        for k in range(PAIRS):
            both = mm(sides[k], named)
            total = jnp.where(place == 2 * k, both[:width], total)
            total = jnp.where(place == 2 * k + 1, both[width:], total)
        pieces.append(total)
    return jnp.concatenate(pieces, axis=1)


def slots_to_messages(values, owner, rank, message_ref):
    slots = owner.shape[1]
    devices = message_ref.shape[0] // PAIRS
    high, low = split(values)
    named = one_hot(lax.broadcasted_iota(jnp.int32, (devices, slots), 0) == owner)
    for k in range(PAIRS):
        first = one_hot(rank == 2 * k)
        second = one_hot(rank == 2 * k + 1)
        placed = jnp.concatenate([high * first, high * second, low * first, low * second], axis=0)
        both = mm_nt(named, placed)
        message_ref[message_rows(k, devices), :] = both[:, :LANES] + both[:, LANES:]


def restrict_kernel(message_ref, owner_ref, rank_ref, weight_ref, prim_ref, vector_ref, out_ref, contrib_ref):
    slots = owner_ref.shape[1]
    restricted = slots_from_messages(message_ref, owner_ref[...], rank_ref[...]) * weight_ref[...]
    out_ref[...] = restricted
    nprim = prim_ref.shape[0]
    chosen = jnp.where(
        lax.broadcasted_iota(jnp.int32, (nprim, slots), 1) == prim_ref[...], 1.0, 0.0
    )
    at_prim = mm_nt(restricted, chosen, HIGH)
    contrib = jnp.sum(at_prim * vector_ref[...], axis=0, keepdims=True)
    wide = jnp.concatenate([contrib, jnp.zeros((1, LANES - nprim), F32)], axis=1)
    contrib_ref[...] = jnp.broadcast_to(wide, contrib_ref.shape)


def correct_kernel(
    neumann_ref, gathered_ref, inverse_ref, owner_ref, rank_ref, weight_ref, prim_ref, vector_ref, message_ref, *, span
):
    slots = owner_ref.shape[1]
    nprim = prim_ref.shape[0]
    devices = gathered_ref.shape[0]
    streams = devices // span
    ncs = inverse_ref.shape[1]
    contrib = gathered_ref[...][:, :nprim]
    lane = lax.broadcasted_iota(jnp.int32, (nprim, ncs), 1)
    spread = jnp.where(lax.rem(lane, nprim) == lax.broadcasted_iota(jnp.int32, (nprim, ncs), 0), 1.0, 0.0)
    tiled = jnp.dot(contrib, spread, precision=HIGH, preferred_element_type=F32)
    device = lax.broadcasted_iota(jnp.int32, (devices, ncs), 0)
    stream = lax.broadcasted_iota(jnp.int32, (devices, ncs), 1)
    mine = lax.div(device, span) == lax.div(stream, nprim)
    coarse_rhs = jnp.sum(jnp.where(mine, tiled, 0.0), axis=0, keepdims=True)
    coarse_sol = jnp.sum(inverse_ref[...] * coarse_rhs, axis=1, keepdims=True)
    chosen = jnp.where(
        lax.broadcasted_iota(jnp.int32, (nprim, slots), 1) == prim_ref[...], coarse_sol, 0.0
    )
    correction = jnp.dot(vector_ref[...], chosen, precision=HIGH, preferred_element_type=F32)
    corrected = (neumann_ref[...] + correction) * weight_ref[...]
    slots_to_messages(corrected, owner_ref[...], rank_ref[...], message_ref)


def restore_kernel(message_ref, owner_ref, rank_ref, index_ref, out_ref, gathered_ref):
    restored = slots_from_messages(message_ref, owner_ref[...], rank_ref[...])
    out_ref[...] = restored
    width, slots = restored.shape
    kc, inner = index_ref.shape
    both = jnp.concatenate(split(restored), axis=0)
    for k in range(kc):
        chosen = one_hot(lax.broadcasted_iota(jnp.int32, (slots, inner), 0) == index_ref[k : k + 1, :])
        got = mm(both, chosen)
        gathered_ref[k] = got[:width] + got[width:]


def image_kernel(backward_ref, restored_ref, diagonal_ref, owner_ref, rank_ref, index_ref, message_ref):
    width, slots = restored_ref.shape
    kc, inner = index_ref.shape
    value = diagonal_ref[...] * restored_ref[...]
    for k in range(kc):
        both = jnp.concatenate(split(backward_ref[k]), axis=0)
        chosen = one_hot(lax.broadcasted_iota(jnp.int32, (slots, inner), 0) == index_ref[k : k + 1, :])
        got = mm_nt(both, chosen)
        value = value - (got[:width] + got[width:])
    slots_to_messages(value, owner_ref[...], rank_ref[...], message_ref)


def rows_to_messages(values, asked, message_ref):
    width, rows = values.shape
    devices = asked.shape[1]
    both = jnp.concatenate(split(values), axis=0)
    place = lax.broadcasted_iota(jnp.int32, (rows, devices), 0)
    for k in range(PAIRS):
        chosen = jnp.concatenate(
            [one_hot(place == asked[2 * k : 2 * k + 1]), one_hot(place == asked[2 * k + 1 : 2 * k + 2])], axis=1
        )
        got = mm(both, chosen)
        got = got[:width] + got[width:]
        stacked = jnp.concatenate([got[:, :devices], got[:, devices:]], axis=0)
        message_ref[message_rows(k, devices), :] = stacked.T


def rows_from_messages(message_ref, asked, rows):
    devices = asked.shape[1]
    width = LANES // 2
    place = lax.broadcasted_iota(jnp.int32, (rows, devices), 0)
    totals = [jnp.zeros((rows, 2 * LANES), F32), jnp.zeros((rows, 2 * LANES), F32)]
    for k in range(0, PAIRS, 2):
        parts = []
        for step in (k, k + 1):
            parts.append(jnp.concatenate(split(message_ref[message_rows(step, devices), :]), axis=1))
        parts = jnp.concatenate(parts, axis=0)
        for side in range(2):
            a, b = 2 * k + side, 2 * k + 2 + side
            chosen = jnp.concatenate(
                [one_hot(place == asked[a : a + 1]), one_hot(place == asked[b : b + 1])], axis=1
            )
            totals[side] = totals[side] + mm(chosen, parts)
    sides = [t[:, :LANES] + t[:, LANES:] for t in totals]
    lane = lax.broadcasted_iota(jnp.int32, (rows, LANES), 1)
    both = jnp.where(lane < width, sides[0], sides[1]).T
    return both[:width] + both[width:]


def fetch_kernel(request_ref, vector_ref, asked_ref, message_ref):
    asked = request_ref[...].astype(F32).T.astype(jnp.int32)[: 2 * PAIRS]
    asked_ref[...] = asked
    rows_to_messages(vector_ref[...], asked, message_ref)


def assemble_kernel(arrived_ref, asked_ref, message_ref, *, rows):
    asked = asked_ref[...]
    assembled = rows_from_messages(arrived_ref, asked, rows)
    rows_to_messages(assembled, asked, message_ref)


def two_sum(a, b):
    total = a + b
    back = total - a
    return total, (a - (total - back)) + (b - back)


def pair_add(a, b):
    total, rest = two_sum(a[0], b[0])
    return total, rest + (a[1] + b[1])


def final_kernel(arrived_ref, asked_ref, basis_ref, image_ref, stats_ref):
    kb, width, rows = basis_ref.shape
    image = rows_from_messages(arrived_ref, asked_ref[...], rows)
    image_ref[...] = image
    fields = [image] + [basis_ref[k] for k in range(kb)]
    quantities = []
    for i in range(1 + kb):
        for j in range(i, 1 + kb):
            product = fields[i] * fields[j]
            pair = (jnp.zeros((8, LANES), F32), jnp.zeros((8, LANES), F32))
            for a in range(0, width, 8):
                for b in range(0, rows, LANES):
                    total, rest = two_sum(pair[0], product[a : a + 8, b : b + LANES])
                    pair = (total, pair[1] + rest)
            for shift in (4, 2, 1):
                pair = pair_add(pair, tuple(pltpu.roll(p, shift, 0) for p in pair))
            quantities.append(pair)
    row = lax.broadcasted_iota(jnp.int32, (8, LANES), 0)
    tiles = []
    for base in range(0, len(quantities), 8):
        tile = (jnp.zeros((8, LANES), F32), jnp.zeros((8, LANES), F32))
        for n, pair in enumerate(quantities[base : base + 8]):
            tile = tuple(jnp.where(row == n, p, t) for p, t in zip(pair, tile))
        shift = LANES // 2
        while shift:
            tile = pair_add(tile, tuple(pltpu.roll(t, shift, 1) for t in tile))
            shift //= 2
        tiles.append(tile)
    pad = [jnp.zeros((LANES - 16 * len(tiles), LANES), F32)]
    square = jnp.concatenate([t[0] for t in tiles] + [t[1] for t in tiles] + pad, axis=0)
    stats_ref[...] = square.T


def finish_kernel(gathered_ref, image_ref, basis_ref, direction_ref, coeff_ref, *, entries):
    kb = basis_ref.shape[0]
    devices = gathered_ref.shape[0]
    count = (kb + 1) * (kb + 2) // 2
    tiles = -(-count // 8)
    values = gathered_ref[...]
    high = values
    low = pltpu.roll(values, LANES - 8 * tiles, 1)
    half = devices // 2
    pair = (high, low)
    while half >= 1:
        pair = pair_add(
            tuple(p[:half] for p in pair), tuple(p[half : 2 * half] for p in pair)
        )
        half //= 2
    lane = lax.broadcasted_iota(jnp.int32, (1, LANES), 1)

    def entry(n):
        return tuple(jnp.sum(jnp.where(lane == n, p, 0.0), axis=1, keepdims=True) for p in pair)

    numbers = [entry(n) for n in range(count)]
    inv_root = 1.0 / math.sqrt(entries)
    projected = [(numbers[1 + k][0] + numbers[1 + k][1]) * inv_root for k in range(kb)]
    steps = [p * inv_root for p in projected]

    def add_product(total, factor, number):
        a, b = factor, number[0]
        a_high = a * 4097.0
        a_high = a_high - (a_high - a)
        b_high = b * 4097.0
        b_high = b_high - (b_high - b)
        a_low, b_low = a - a_high, b - b_high
        product = a * b
        rest = ((a_high * b_high - product) + a_high * b_low + a_low * b_high) + a_low * b_low
        return pair_add(total, (product, rest + factor * number[1]))

    def scaled(number, factor):
        zero = jnp.zeros_like(factor)
        return add_product((zero, zero), factor, number)

    total = numbers[0]
    at = 1 + kb
    for k in range(kb):
        total = add_product(total, -2.0 * steps[k], numbers[1 + k])
    for k in range(kb):
        for other in range(k, kb):
            factor = steps[k] if other == k else 2.0 * steps[k]
            total = add_product(total, factor, scaled(numbers[at], steps[other]))
            at += 1
    squares = jnp.maximum(total[0] + total[1], 0.0)
    root_mean = jnp.sqrt(squares / entries + 1e-06)
    remainder = image_ref[...]
    for k in range(kb):
        remainder = remainder - steps[k] * basis_ref[k]
    direction_ref[...] = remainder / root_mean
    coeffs = jnp.zeros((1, LANES), F32)
    for n, value in enumerate(projected + [root_mean]):
        coeffs = jnp.where(lane == n, value, coeffs)
    coeff_ref[...] = coeffs


def body(
    basis,
    interface_row_owner,
    interface_local_row,
    interface_slot_weight,
    local_inverse,
    prim_index,
    prim_vector,
    coarse_inverse,
    interface_shifted_diagonal,
    coupling_index,
    coupling_blocks,
    interior_inverse,
):
    span = lax.axis_size("span")
    devices = lax.axis_size("stream") * span
    kb, width, rows = basis.shape
    slots = interface_local_row.shape[0]
    kc, inner = coupling_index.shape
    nprim = prim_index.shape[0]
    entries = width * rows * devices
    owner = interface_row_owner.reshape(1, slots)
    row = interface_local_row.reshape(1, slots)
    weight = interface_slot_weight.reshape(1, slots)
    prim = prim_index.reshape(nprim, 1)
    shape = jax.ShapeDtypeStruct
    message = shape((devices * PAIRS, LANES), F32)
    field = shape((width, slots), F32)
    square = shape((devices, LANES), F32)

    def exchange(x, per):
        sent = x.reshape(devices, per, LANES)
        return lax.all_to_all(sent, ("stream", "span"), split_axis=0, concat_axis=0, tiled=True).reshape(x.shape)

    requests, rank = call(
        plan_kernel, (shape((devices, LANES), jnp.int32), shape((1, slots), jnp.int32)), owner, row
    )
    arrived = exchange(requests, 1)
    asked, sent = call(fetch_kernel, (shape((2 * PAIRS, devices), jnp.int32), message), arrived, basis[kb - 1])
    restricted, contrib = call(
        restrict_kernel, (field, square), exchange(sent, PAIRS), owner, rank, weight, prim, prim_vector
    )
    contribs = exchange(contrib, 1)
    neumann_piece = jnp.sum(local_inverse * restricted[None, :, :], axis=1)
    sent = call(
        functools.partial(correct_kernel, span=span),
        message,
        neumann_piece,
        contribs,
        coarse_inverse,
        owner,
        rank,
        weight,
        prim,
        prim_vector,
    )
    sent = call(functools.partial(assemble_kernel, rows=rows), message, exchange(sent, PAIRS), asked)
    restored, gathered = call(
        restore_kernel,
        (field, shape((kc, width, inner), F32)),
        exchange(sent, PAIRS),
        owner,
        rank,
        coupling_index,
    )
    interior_in = jnp.sum(coupling_blocks * gathered[:, None, :, :], axis=(0, 2))
    interior_sol = jnp.sum(interior_inverse * interior_in[None, :, :], axis=1)
    backward = jnp.sum(coupling_blocks * interior_sol[None, :, None, :], axis=1)
    sent = call(
        image_kernel,
        message,
        backward,
        restored,
        interface_shifted_diagonal,
        owner,
        rank,
        coupling_index,
    )
    image, stats = call(
        final_kernel, (shape((width, rows), F32), square), exchange(sent, PAIRS), asked, basis
    )
    direction, coeffs = call(
        functools.partial(finish_kernel, entries=entries),
        (shape((width, rows), F32), shape((1, LANES), F32)),
        exchange(stats, 1),
        image,
        basis,
    )
    return direction, coeffs[0, : kb + 1]


def solution(mesh):
    placed = (
        P(None, None, ("stream", "span")),
        P(("stream", "span"), None),
        P(("stream", "span")),
        P(("stream", "span")),
        P(None, None, ("stream", "span")),
        P(("stream", "span")),
        P(None, ("stream", "span")),
        P("stream", None),
        P(None, ("stream", "span")),
        P(None, ("stream", "span")),
        P(None, None, None, ("stream", "span")),
        P(None, None, ("stream", "span")),
    )
    return jax.shard_map(
        body,
        mesh=mesh,
        in_specs=placed,
        out_specs=(P(None, ("stream", "span")), P()),
        check_vma=False,
    )
```

profile of v0, /device:TPU:1, one launch (start us, length us, event | category | flops | bytes accessed | tf_op | source)
XLA Modules:
  0.0 149.0 jit_solution(14137685021745089202)
XLA Ops:
  0.7 0.7 copy-done.3
  1.4 0.7 copy-done.9
  2.1 1.2 shard_map.131
  3.2 11.5 %all-to-all-start = ((s32[128,1,128]{2,1,0:T(1,128)}), s32[128,1,128]{2,1,0:T(1,128)S(1)}, u32[]{:S(2)}, u32[]{:S(2)}) async-start(s32[128,1,128]{2,1,0:T(1,128)} %bitcast.3), calls=%async_computation | async-start | bytes 131072 | tf_op jit(solution)/shard_map/all_to_all | solution.py:359
  14.7 0.9 slice_bitcast_fusion.vector_ref
  15.7 8.9 %all-to-all-done = s32[128,1,128]{2,1,0:T(1,128)S(1)} async-done(((s32[128,1,128]{2,1,0:T(1,128)}), s32[128,1,128]{2,1,0:T(1,128)S(1)}, u32[]{:S(2)}, u32[]{:S(2)}) %all-to-all-start) | async-done | bytes 65568 | tf_op jit(solution)/shard_map/all_to_all | solution.py:359
  24.5 1.4 shard_map.132
  25.9 4.0 %all-to-all-start.1 = ((f32[128,8,128]{2,1,0:T(8,128)}), f32[128,8,128]{2,1,0:T(8,128)S(1)}, u32[]{:S(2)}, u32[]{:S(2)}) async-start(f32[128,8,128]{2,1,0:T(8,128)} %bitcast.6), calls=%async_computation.1 | async-start | bytes 1048576 | tf_op jit(solution)/shard_map/all_to_all | solution.py:359
  29.9 0.8 copy.20.vector_ref
  30.7 0.7 copy.19.prim_ref
  31.4 12.6 %all-to-all-done.1 = f32[128,8,128]{2,1,0:T(8,128)S(1)} async-done(((f32[128,8,128]{2,1,0:T(8,128)}), f32[128,8,128]{2,1,0:T(8,128)S(1)}, u32[]{:S(2)}, u32[]{:S(2)}) %all-to-all-start.1) | async-done | bytes 524320 | tf_op jit(solution)/shard_map/all_to_all | solution.py:359
  44.0 0.7 copy-done.4
  44.7 0.7 copy-done.6
  45.4 1.8 %shard_map.133 = (f32[64,1024]{1,0:T(8,128)S(1)}, f32[128,128]{1,0:T(8,128)}) custom-call(f32[1024,128]{1,0:T(8,128)S(1)} %bitcast.28, s32[1,1024]{1,0:T(1,128)S(1)} %bitcast.39, s32[1,1024]{1,0:T(1,128)S(1)} %get-tuple-element.16.rank_ref, f32[1,1024]{1,0:T(1,128)S(1)} %bitcast.44, s32[32,1]{1,0:T(8,128)S(1)} %copy.19.prim_ref, f32[64,32]{1,0:T(8,128)S(1)} %copy.20.vector_ref), custom_call_target="tpu_custom_call" | custom-call | tf_op jit(solution)/shard_map/pallas_call | solution.py:40
  47.2 3.6 %all-to-all-start.2 = ((f32[128,1,128]{2,1,0:T(1,128)}), f32[128,1,128]{2,1,0:T(1,128)S(1)}, u32[]{:S(2)}, u32[]{:S(2)}) async-start(f32[128,1,128]{2,1,0:T(1,128)} %bitcast.11), calls=%async_computation.2 | async-start | bytes 131072 | tf_op jit(solution)/shard_map/all_to_all | solution.py:359
  50.9 6.2 %multiply_reduce_fusion.neumann_ref = f32[64,1024]{1,0:T(8,128)S(1)} fusion(bf16[64,64,1024]{2,1,0:T(8,128)(2,1)} %param.16, f32[64,1024]{1,0:T(8,128)S(1)} %get-tuple-element.17), kind=kLoop, calls=%fused_computation.4 | loop fusion | flops 12517376 | bytes 8912896 | tf_op jit(solution)/shard_map/reduce_sum | solution.py:370
  57.0 3.8 %all-to-all-done.2 = f32[128,1,128]{2,1,0:T(1,128)S(1)} async-done(((f32[128,1,128]{2,1,0:T(1,128)}), f32[128,1,128]{2,1,0:T(1,128)S(1)}, u32[]{:S(2)}, u32[]{:S(2)}) %all-to-all-start.2) | async-done | bytes 65568 | tf_op jit(solution)/shard_map/all_to_all | solution.py:359
  60.8 2.4 %shard_map.134 = f32[1024,128]{1,0:T(8,128)S(1)} custom-call(f32[64,1024]{1,0:T(8,128)S(1)} %multiply_reduce_fusion.neumann_ref, f32[128,128]{1,0:T(8,128)S(1)} %bitcast.35, f32[32,1024]{1,0:T(8,128)S(1)} %copy-done.2, s32[1,1024]{1,0:T(1,128)S(1)} %bitcast.40, s32[1,1024]{1,0:T(1,128)S(1)} %get-tuple-element.16.rank_ref, f32[1,1024]{1,0:T(1,128)S(1)} %bitcast.45, ...), custom_call_target="tpu_custom_call" | custom-call | tf_op jit(solution)/shard_map/pallas_call | solution.py:40
  63.3 20.1 %all_to_all.35 = f32[128,8,128]{2,1,0:T(8,128)S(1)} all-to-all(f32[128,8,128]{2,1,0:T(8,128)S(1)} %bitcast.29), channel_id=1, replica_groups=mesh['stream'=32,'span'=4] {'stream','span'}, dimensions={0} | all-to-all | bytes 1048576 | tf_op jit(solution)/shard_map/all_to_all | solution.py:359
  83.4 1.3 shard_map.135
  84.7 17.5 %all_to_all.36 = f32[128,8,128]{2,1,0:T(8,128)S(1)} all-to-all(f32[128,8,128]{2,1,0:T(8,128)S(1)} %bitcast.34), channel_id=1, replica_groups=mesh['stream'=32,'span'=4] {'stream','span'}, dimensions={0} | all-to-all | bytes 1048576 | tf_op jit(solution)/shard_map/all_to_all | solution.py:359
  102.2 1.4 shard_map.136
  103.6 0.0 slice-start.1
  103.6 5.7 %fusion = f32[64,512]{1,0:T(8,128)S(1)} fusion(bf16[2,64,64,512]{3,2,1,0:T(8,128)(2,1)} %param.22, f32[2,64,512]{2,1,0:T(8,128)S(1)} %get-tuple-element.20), kind=kLoop, calls=%fused_computation.2 | loop fusion | flops 12550144 | bytes 8781824 | tf_op jit(solution)/shard_map/reduce_sum | solution.py:392
  109.3 1.4 multiply_reduce_fusion.1
  110.7 2.0 %fusion.1.backward_ref = f32[2,64,512]{2,1,0:T(8,128)S(1)} fusion(bf16[2,64,64,512]{3,2,1,0:T(8,128)(2,1)S(1)} %bitcast.48, f32[64,512]{1,0:T(8,128)S(1)} %multiply_reduce_fusion.1), kind=kLoop, calls=%fused_computation.3 | loop fusion | flops 12517376 | bytes 8781824 | tf_op jit(solution)/shard_map/reduce_sum | solution.py:394
  112.7 2.2 %shard_map.137 = f32[1024,128]{1,0:T(8,128)S(1)} custom-call(f32[2,64,512]{2,1,0:T(8,128)S(1)} %fusion.1.backward_ref, f32[64,1024]{1,0:T(8,128)S(1)} %get-tuple-element.21.restored_ref, f32[64,1024]{1,0:T(8,128)S(1)} %copy-done.1, s32[1,1024]{1,0:T(1,128)S(1)} %bitcast.42, s32[1,1024]{1,0:T(1,128)S(1)} %get-tuple-element.16.rank_ref, s32[2,512]{1,0:T(2,128)S(1)} %copy-done.8), custom_call_target="tpu_custom_call" | custom-call | tf_op jit(solution)/shard_map/pallas_call | solution.py:40
  114.9 17.5 %all_to_all.37 = f32[128,8,128]{2,1,0:T(8,128)S(1)} all-to-all(f32[128,8,128]{2,1,0:T(8,128)S(1)} %bitcast.32), channel_id=1, replica_groups=mesh['stream'=32,'span'=4] {'stream','span'}, dimensions={0} | all-to-all | bytes 1048576 | tf_op jit(solution)/shard_map/all_to_all | solution.py:359
  132.4 1.9 %shard_map.138 = (f32[64,512]{1,0:T(8,128)S(1)}, f32[128,128]{1,0:T(8,128)S(1)}) custom-call(f32[1024,128]{1,0:T(8,128)S(1)} %bitcast.30, s32[16,128]{1,0:T(8,128)S(1)} %get-tuple-element.19.asked_ref, f32[4,64,512]{2,1,0:T(8,128)S(1)} %copy-done), custom_call_target="tpu_custom_call" | custom-call | tf_op jit(solution)/shard_map/pallas_call | solution.py:40
  134.3 13.2 %all_to_all.38 = f32[128,1,128]{2,1,0:T(1,128)S(1)} all-to-all(f32[128,1,128]{2,1,0:T(1,128)S(1)} %bitcast.43), channel_id=1, replica_groups=mesh['stream'=32,'span'=4] {'stream','span'}, dimensions={0} | all-to-all | bytes 131072 | tf_op jit(solution)/shard_map/all_to_all | solution.py:359
  147.5 1.0 shard_map.139
  148.5 0.5 slice_bitcast_fusion.1
  (22 shorter events, 0.1 us)
Async XLA Ops:
  0.6 60.2 %copy-start.2 = (f32[32,1024]{1,0:T(8,128)S(1)}, f32[32,1024]{1,0:T(8,128)}, u32[]{:S(2)}) copy-start(f32[32,1024]{1,0:T(8,128)} %inverse_ref.1) | copy-start | bytes 393220
  0.6 0.7 copy-start.3
  1.4 0.7 copy-start.9
  2.1 58.8 %copy-start.5 = (s32[1024,1]{0,1:T(1,128)S(1)}, s32[1024,1]{0,1:T(1,128)}, u32[]{:S(2)}) copy-start(s32[1024,1]{0,1:T(1,128)} %param.13) | copy-start | bytes 12292
  2.1 58.8 %copy-start.7 = (f32[1024]{0:T(1024)S(1)}, f32[1024]{0:T(1024)}, u32[]{:S(2)}) copy-start(f32[1024]{0:T(1024)} %param.15) | copy-start | bytes 12292
  2.1 100.1 %copy-start.8 = (s32[2,512]{1,0:T(2,128)S(1)}, s32[2,512]{1,0:T(2,128)}, u32[]{:S(2)}) copy-start(s32[2,512]{1,0:T(2,128)} %index_ref.3) | copy-start | bytes 12292
  3.2 21.3 %all-to-all-start = ((s32[128,1,128]{2,1,0:T(1,128)}), s32[128,1,128]{2,1,0:T(1,128)S(1)}, u32[]{:S(2)}, u32[]{:S(2)}) async-start(s32[128,1,128]{2,1,0:T(1,128)} %bitcast.3), calls=%async_computation | async-start | bytes 131072 | tf_op jit(solution)/shard_map/all_to_all | solution.py:359
  25.9 18.1 %all-to-all-start.1 = ((f32[128,8,128]{2,1,0:T(8,128)}), f32[128,8,128]{2,1,0:T(8,128)S(1)}, u32[]{:S(2)}, u32[]{:S(2)}) async-start(f32[128,8,128]{2,1,0:T(8,128)} %bitcast.6), calls=%async_computation.1 | async-start | bytes 1048576 | tf_op jit(solution)/shard_map/all_to_all | solution.py:359
  44.0 0.7 copy-start.4
  44.7 0.7 copy-start.6
  47.2 13.6 %all-to-all-start.2 = ((f32[128,1,128]{2,1,0:T(1,128)}), f32[128,1,128]{2,1,0:T(1,128)S(1)}, u32[]{:S(2)}, u32[]{:S(2)}) async-start(f32[128,1,128]{2,1,0:T(1,128)} %bitcast.11), calls=%async_computation.2 | async-start | bytes 131072 | tf_op jit(solution)/shard_map/all_to_all | solution.py:359
  60.8 48.4 %copy-start.10 = (bf16[64,64,512]{2,1,0:T(8,128)(2,1)S(1)}, bf16[64,64,512]{2,1,0:T(8,128)(2,1)}, u32[]{:S(2)}) copy-start(bf16[64,64,512]{2,1,0:T(8,128)(2,1)} %param.23) | copy-start | bytes 12582916
  63.2 47.4 %slice-start = ((s8[8388608]{0:T(1024)(128)(4,1)}), s8[4194304]{0:T(1024)(128)(4,1)S(1)}, s32[]{:S(2)}) async-start(s8[8388608]{0:T(1024)(128)(4,1)} %bitcast.47), calls=%async_computation.7 | async-start | bytes 8388608
  103.6 7.1 %slice-start.1 = ((s8[8388608]{0:T(1024)(128)(4,1)}), s8[4194304]{0:T(1024)(128)(4,1)S(1)}, s32[]{:S(2)}) async-start(s8[8388608]{0:T(1024)(128)(4,1)} %bitcast.47), calls=%async_computation.8 | async-start | bytes 8388608
  109.2 3.5 %copy-start.1 = (f32[64,1024]{1,0:T(8,128)S(1)}, f32[64,1024]{1,0:T(8,128)}, u32[]{:S(2)}) copy-start(f32[64,1024]{1,0:T(8,128)} %diagonal_ref.1) | copy-start | bytes 786436
  109.2 23.2 %copy-start = (f32[4,64,512]{2,1,0:T(8,128)S(1)}, f32[4,64,512]{2,1,0:T(8,128)}, u32[]{:S(2)}) copy-start(f32[4,64,512]{2,1,0:T(8,128)} %basis_ref.3) | copy-start | bytes 1572868
where the time goes:
time: 150 us; the launch traced here: 149 us
  blocking collectives  68.3 us (46%)
  waiting for transfers between devices  25.3 us (17%)
  starting transfers between devices  19.1 us (13%)
  other arithmetic  15.2 us (10%)
  Pallas kernels  14.5 us (10%)
  local copies, waits for them, and re-layouts  5.79 us (4%)
    all_to_all x4, blocking collectives, exchange(): lax.all_to_all(sent, ('stream', 'span'), split_axis=0, concat_axis=0, til...  68.3 us
    all_to_all x3, waiting for transfers between devices, exchange(): lax.all_to_all(sent, ('stream', 'span'), split_axis=0, concat_axis=0, til...  25.3 us
    all_to_all x3, starting transfers between devices, exchange(): lax.all_to_all(sent, ('stream', 'span'), split_axis=0, concat_axis=0, til...  19.1 us
    pallas_call x9, Pallas kernels, call(): pl.pallas_call(kernel, out_shape=out_shape, compiler_params=pltpu.Compile...  14.5 us
    reduce_sum x1, other arithmetic, body(): neumann_piece = jnp.sum(local_inverse * restricted[None, :, :], axis=1)  6.16 us
    reduce_sum x1, other arithmetic, body(): jnp.sum(coupling_blocks * gathered[:, None, :, :], axis=(0, 2))  5.65 us
    unnamed x27, local copies, waits for them, and re-layouts  3.62 us
  transfers between devices with their start and end apart: 3, of which 3 were waited for; matrix products, arithmetic and copies ran while one was open for 6% of the time, Pallas kernels for 0%

commit v1 on v0

--- a/solution.py
+++ b/solution.py
@@ -45,9 +45,17 @@
     )(*args)
 
 
-def plan_kernel(owner_ref, row_ref, request_ref, rank_ref):
+def plan_kernel(owner_hbm, row_hbm, request_ref, ids_ref, owner_ref, row_ref, sems):
     slots = owner_ref.shape[1]
     devices = request_ref.shape[0]
+    copies = [
+        pltpu.make_async_copy(owner_hbm, owner_ref, sems.at[0]),
+        pltpu.make_async_copy(row_hbm, row_ref, sems.at[1]),
+    ]
+    for copy in copies:
+        copy.start()
+    for copy in copies:
+        copy.wait()
     owner = owner_ref[...]
     row = row_ref[...]
     named = one_hot(lax.broadcasted_iota(jnp.int32, (devices, slots), 0) == owner)
@@ -63,7 +71,8 @@
         ranks.append(jnp.sum((counts[:, :LANES] + carry) * part.astype(F32), axis=0, keepdims=True))
         carry = carry + counts[:, LANES:]
     rank = jnp.concatenate(ranks, axis=1).astype(jnp.int32)
-    rank_ref[...] = rank
+    ids_ref[0:1, :] = owner
+    ids_ref[1:2, :] = rank
     at_rank = lax.broadcasted_iota(jnp.int32, (LANES, slots), 0) == rank
     tens = jnp.where(at_rank, (row >> 4).astype(F32), 0.0).astype(BF16)
     units = jnp.where(at_rank, (row & 15).astype(F32), 0.0).astype(BF16)
@@ -107,27 +116,98 @@
         message_ref[message_rows(k, devices), :] = both[:, :LANES] + both[:, LANES:]
 
 
-def restrict_kernel(message_ref, owner_ref, rank_ref, weight_ref, prim_ref, vector_ref, out_ref, contrib_ref):
-    slots = owner_ref.shape[1]
-    restricted = slots_from_messages(message_ref, owner_ref[...], rank_ref[...]) * weight_ref[...]
+def block_sums(block_refs, vectors, a, lanes):
+    total = None
+    for ref, vector in zip(block_refs, vectors):
+        product = ref[a, :, lanes].astype(F32) * vector
+        part = jnp.sum(product.reshape(product.shape[0] // 8, 8, LANES), axis=0)
+        total = part if total is None else total + part
+    for shift in (4, 2, 1):
+        total = total + pltpu.roll(total, shift, 0)
+    return total
+
+
+def apply_blocks(block_refs, vector_refs, out_ref, c):
+    width = out_ref.shape[0]
+    row = lax.broadcasted_iota(jnp.int32, (8, LANES), 0)
+    lanes = slice(c * LANES, (c + 1) * LANES)
+    vectors = [ref[:, lanes] for ref in vector_refs]
+
+    def rows_of(tile, _):
+        first = pl.multiple_of(tile * 8, 8)
+        result = jnp.zeros((8, LANES), F32)
+        for j in range(8):
+            result = jnp.where(row == j, block_sums(block_refs, vectors, first + j, lanes), result)
+        out_ref[pl.ds(first, 8), lanes] = result
+        return 0
+
+    lax.fori_loop(0, width // 8, rows_of, 0)
+
+
+def prepare_kernel(
+    ids_ref,
+    weight_ref,
+    prim_ref,
+    vector_ref,
+    basis_ref,
+    weights_ref,
+    chosen_ref,
+    vectors_ref,
+    coarse_ref,
+    named_ref,
+    gram_ref,
+    last_ref,
+):
+    slots = ids_ref.shape[1]
+    nprim = prim_ref.shape[0]
+    devices = named_ref.shape[0]
+    chosen = lax.broadcasted_iota(jnp.int32, (nprim, slots), 1) == prim_ref[...]
+    weights_ref[...] = weight_ref[...]
+    chosen_ref[...] = jnp.where(chosen, 1.0, 0.0)
+    vectors_ref[...] = vector_ref[...]
+
+    def column(values):
+        return jnp.sum(jnp.where(chosen, values.astype(F32), 0.0), axis=1, keepdims=True)
+
+    weight, rank, owner = column(weight_ref[...]), column(ids_ref[1:2, :]), column(ids_ref[0:1, :])
+    named_ref[...] = one_hot(
+        lax.broadcasted_iota(jnp.int32, (nprim, devices), 1).astype(F32) == owner
+    ).astype(F32).T.astype(BF16)
+    vectors = vector_ref[...].T * weight
+    for k in range(PAIRS):
+        sides = [jnp.where(rank == 2.0 * k + side, vectors, 0.0) for side in range(2)]
+        coarse_ref[k * nprim : (k + 1) * nprim, :] = jnp.concatenate(sides, axis=1)
+    kb = basis_ref.shape[0]
+    fields = [basis_ref[k] for k in range(kb)]
+    last_ref[...] = fields[kb - 1]
+    store_sums([(fields[i], fields[j]) for i in range(kb) for j in range(i, kb)], gram_ref)
+
+
+def restrict_kernel(message_ref, ids_ref, weight_ref, chosen_ref, vector_ref, out_ref, contrib_ref):
+    restricted = slots_from_messages(message_ref, ids_ref[0:1, :], ids_ref[1:2, :]) * weight_ref[...]
     out_ref[...] = restricted
-    nprim = prim_ref.shape[0]
-    chosen = jnp.where(
-        lax.broadcasted_iota(jnp.int32, (nprim, slots), 1) == prim_ref[...], 1.0, 0.0
-    )
-    at_prim = mm_nt(restricted, chosen, HIGH)
+    at_prim = mm_nt(restricted, chosen_ref[...], HIGH)
     contrib = jnp.sum(at_prim * vector_ref[...], axis=0, keepdims=True)
-    wide = jnp.concatenate([contrib, jnp.zeros((1, LANES - nprim), F32)], axis=1)
+    wide = jnp.concatenate([contrib, jnp.zeros((1, LANES - contrib.shape[1]), F32)], axis=1)
     contrib_ref[...] = jnp.broadcast_to(wide, contrib_ref.shape)
 
 
-def correct_kernel(
-    neumann_ref, gathered_ref, inverse_ref, owner_ref, rank_ref, weight_ref, prim_ref, vector_ref, message_ref, *, span
-):
-    slots = owner_ref.shape[1]
-    nprim = prim_ref.shape[0]
-    devices = gathered_ref.shape[0]
-    streams = devices // span
+def neumann_kernel(blocks_hbm, restricted_ref, ids_ref, weight_ref, message_ref, piece_ref, blocks_ref, sems):
+    columns = piece_ref.shape[1]
+    copies = []
+    for c in range(columns // LANES):
+        lanes = pl.ds(c * LANES, LANES)
+        copies.append(pltpu.make_async_copy(blocks_hbm.at[:, :, lanes], blocks_ref.at[:, :, lanes], sems.at[c]))
+    for copy in copies:
+        copy.start()
+    for c, copy in enumerate(copies):
+        copy.wait()
+        apply_blocks([blocks_ref], [restricted_ref], piece_ref, c)
+    slots_to_messages(piece_ref[...] * weight_ref[...], ids_ref[0:1, :], ids_ref[1:2, :], message_ref)
+
+
+def correct_kernel(packed_ref, gathered_ref, inverse_ref, coarse_ref, named_ref, message_ref, *, span):
+    devices, nprim = named_ref.shape
     ncs = inverse_ref.shape[1]
     contrib = gathered_ref[...][:, :nprim]
     lane = lax.broadcasted_iota(jnp.int32, (nprim, ncs), 1)
@@ -138,36 +218,78 @@
     mine = lax.div(device, span) == lax.div(stream, nprim)
     coarse_rhs = jnp.sum(jnp.where(mine, tiled, 0.0), axis=0, keepdims=True)
     coarse_sol = jnp.sum(inverse_ref[...] * coarse_rhs, axis=1, keepdims=True)
-    chosen = jnp.where(
-        lax.broadcasted_iota(jnp.int32, (nprim, slots), 1) == prim_ref[...], coarse_sol, 0.0
-    )
-    correction = jnp.dot(vector_ref[...], chosen, precision=HIGH, preferred_element_type=F32)
-    corrected = (neumann_ref[...] + correction) * weight_ref[...]
-    slots_to_messages(corrected, owner_ref[...], rank_ref[...], message_ref)
-
-
-def restore_kernel(message_ref, owner_ref, rank_ref, index_ref, out_ref, gathered_ref):
-    restored = slots_from_messages(message_ref, owner_ref[...], rank_ref[...])
-    out_ref[...] = restored
+    for k in range(PAIRS):
+        high, low = split(coarse_ref[k * nprim : (k + 1) * nprim, :] * coarse_sol)
+        both = mm(named_ref[...], jnp.concatenate([high, low], axis=1))
+        at = message_rows(k, devices)
+        message_ref[at, :] = packed_ref[at, :] + (both[:, :LANES] + both[:, LANES:])
+
+
+def schur_kernel(
+    arrived_ref,
+    ids_ref,
+    index_ref,
+    diagonal_ref,
+    coupling_hbm,
+    inverse_hbm,
+    message_ref,
+    gathered_ref,
+    inner_ref,
+    backward_ref,
+    coupling_ref,
+    inverse_ref,
+    sems,
+):
+    kc, inner = index_ref.shape
+    chunks = inner // LANES
+    copies = []
+    for c in range(chunks):
+        lanes = pl.ds(c * LANES, LANES)
+        copies.append(
+            pltpu.make_async_copy(coupling_hbm.at[:, :, :, lanes], coupling_ref.at[:, :, :, lanes], sems.at[c, 0])
+        )
+        copies.append(
+            pltpu.make_async_copy(inverse_hbm.at[:, :, lanes], inverse_ref.at[:, :, lanes], sems.at[c, 1])
+        )
+    for copy in copies:
+        copy.start()
+    owner, rank = ids_ref[0:1, :], ids_ref[1:2, :]
+    restored = slots_from_messages(arrived_ref, owner, rank)
     width, slots = restored.shape
-    kc, inner = index_ref.shape
     both = jnp.concatenate(split(restored), axis=0)
     for k in range(kc):
         chosen = one_hot(lax.broadcasted_iota(jnp.int32, (slots, inner), 0) == index_ref[k : k + 1, :])
         got = mm(both, chosen)
         gathered_ref[k] = got[:width] + got[width:]
-
-
-def image_kernel(backward_ref, restored_ref, diagonal_ref, owner_ref, rank_ref, index_ref, message_ref):
-    width, slots = restored_ref.shape
-    kc, inner = index_ref.shape
-    value = diagonal_ref[...] * restored_ref[...]
+    blocks = [coupling_ref.at[k] for k in range(kc)]
+    for c in range(chunks):
+        for copy in copies[2 * c : 2 * c + 2]:
+            copy.wait()
+        apply_blocks(blocks, [gathered_ref.at[k] for k in range(kc)], inner_ref, c)
+        lanes = slice(c * LANES, (c + 1) * LANES)
+        vector = inner_ref[:, lanes]
+
+        def step(tile, totals, lanes=lanes, vector=vector):
+            for j in range(8):
+                a = tile * 8 + j
+                solved = block_sums([inverse_ref], [vector], a, lanes)
+                totals = tuple(
+                    total + ref[a, :, lanes].astype(F32).reshape(width // 8, 8, LANES) * solved[None]
+                    for total, ref in zip(totals, blocks)
+                )
+            return totals
+
+        zero = jnp.zeros((width // 8, 8, LANES), F32)
+        totals = lax.fori_loop(0, width // 8, step, (zero,) * kc)
+        for k in range(kc):
+            backward_ref[k, :, lanes] = totals[k].reshape(width, LANES)
+    value = diagonal_ref[...] * restored
     for k in range(kc):
         both = jnp.concatenate(split(backward_ref[k]), axis=0)
         chosen = one_hot(lax.broadcasted_iota(jnp.int32, (slots, inner), 0) == index_ref[k : k + 1, :])
         got = mm_nt(both, chosen)
         value = value - (got[:width] + got[width:])
-    slots_to_messages(value, owner_ref[...], rank_ref[...], message_ref)
+    slots_to_messages(value, owner, rank, message_ref)
 
 
 def rows_to_messages(values, asked, message_ref):
@@ -230,47 +352,54 @@
     return total, rest + (a[1] + b[1])
 
 
-def final_kernel(arrived_ref, asked_ref, basis_ref, image_ref, stats_ref):
-    kb, width, rows = basis_ref.shape
-    image = rows_from_messages(arrived_ref, asked_ref[...], rows)
-    image_ref[...] = image
-    fields = [image] + [basis_ref[k] for k in range(kb)]
-    quantities = []
-    for i in range(1 + kb):
-        for j in range(i, 1 + kb):
-            product = fields[i] * fields[j]
+def store_sums(products, out_ref):
+    row = lax.broadcasted_iota(jnp.int32, (8, LANES), 0)
+    tiles = []
+    for base in range(0, len(products), 8):
+        tile = (jnp.zeros((8, LANES), F32), jnp.zeros((8, LANES), F32))
+        for n, (left, right) in enumerate(products[base : base + 8]):
+            width, rows = left.shape
             pair = (jnp.zeros((8, LANES), F32), jnp.zeros((8, LANES), F32))
             for a in range(0, width, 8):
                 for b in range(0, rows, LANES):
-                    total, rest = two_sum(pair[0], product[a : a + 8, b : b + LANES])
+                    term = left[a : a + 8, b : b + LANES] * right[a : a + 8, b : b + LANES]
+                    total, rest = two_sum(pair[0], term)
                     pair = (total, pair[1] + rest)
             for shift in (4, 2, 1):
                 pair = pair_add(pair, tuple(pltpu.roll(p, shift, 0) for p in pair))
-            quantities.append(pair)
-    row = lax.broadcasted_iota(jnp.int32, (8, LANES), 0)
-    tiles = []
-    for base in range(0, len(quantities), 8):
-        tile = (jnp.zeros((8, LANES), F32), jnp.zeros((8, LANES), F32))
-        for n, pair in enumerate(quantities[base : base + 8]):
             tile = tuple(jnp.where(row == n, p, t) for p, t in zip(pair, tile))
         shift = LANES // 2
         while shift:
             tile = pair_add(tile, tuple(pltpu.roll(t, shift, 1) for t in tile))
             shift //= 2
         tiles.append(tile)
-    pad = [jnp.zeros((LANES - 16 * len(tiles), LANES), F32)]
-    square = jnp.concatenate([t[0] for t in tiles] + [t[1] for t in tiles] + pad, axis=0)
+    half = out_ref.shape[0] // 2
+    for n, tile in enumerate(tiles):
+        out_ref[n * 8 : (n + 1) * 8, :] = tile[0]
+        out_ref[half + n * 8 : half + (n + 1) * 8, :] = tile[1]
+    for n in range(len(tiles), half // 8):
+        out_ref[n * 8 : (n + 1) * 8, :] = jnp.zeros((8, LANES), F32)
+        out_ref[half + n * 8 : half + (n + 1) * 8, :] = jnp.zeros((8, LANES), F32)
+
+
+def final_kernel(arrived_ref, asked_ref, basis_ref, gram_ref, image_ref, stats_ref, sums_ref):
+    kb, width, rows = basis_ref.shape
+    image = rows_from_messages(arrived_ref, asked_ref[...], rows)
+    image_ref[...] = image
+    store_sums([(image, image)] + [(image, basis_ref[k]) for k in range(kb)], sums_ref)
+    used = sums_ref.shape[0] + gram_ref.shape[0]
+    square = jnp.concatenate([sums_ref[...], gram_ref[...], jnp.zeros((LANES - used, LANES), F32)], axis=0)
     stats_ref[...] = square.T
 
 
 def finish_kernel(gathered_ref, image_ref, basis_ref, direction_ref, coeff_ref, *, entries):
     kb = basis_ref.shape[0]
     devices = gathered_ref.shape[0]
-    count = (kb + 1) * (kb + 2) // 2
-    tiles = -(-count // 8)
-    values = gathered_ref[...]
-    high = values
-    low = pltpu.roll(values, LANES - 8 * tiles, 1)
+    gram = 16
+    high = gathered_ref[...]
+    lane = lax.broadcasted_iota(jnp.int32, high.shape, 1)
+    low = jnp.where(lane < gram, pltpu.roll(high, LANES - 8, 1), pltpu.roll(high, LANES - gram, 1))
+    pair = (high, low)
     half = devices // 2
     pair = (high, low)
     while half >= 1:
@@ -283,7 +412,8 @@
     def entry(n):
         return tuple(jnp.sum(jnp.where(lane == n, p, 0.0), axis=1, keepdims=True) for p in pair)
 
-    numbers = [entry(n) for n in range(count)]
+    numbers = [entry(n) for n in range(1 + kb)]
+    numbers += [entry(gram + n) for n in range(kb * (kb + 1) // 2)]
     inv_root = 1.0 / math.sqrt(entries)
     projected = [(numbers[1 + k][0] + numbers[1 + k][1]) * inv_root for k in range(kb)]
     steps = [p * inv_root for p in projected]
@@ -358,52 +488,94 @@
         sent = x.reshape(devices, per, LANES)
         return lax.all_to_all(sent, ("stream", "span"), split_axis=0, concat_axis=0, tiled=True).reshape(x.shape)
 
-    requests, rank = call(
-        plan_kernel, (shape((devices, LANES), jnp.int32), shape((1, slots), jnp.int32)), owner, row
-    )
-    arrived = exchange(requests, 1)
-    asked, sent = call(fetch_kernel, (shape((2 * PAIRS, devices), jnp.int32), message), arrived, basis[kb - 1])
-    restricted, contrib = call(
-        restrict_kernel, (field, square), exchange(sent, PAIRS), owner, rank, weight, prim, prim_vector
-    )
-    contribs = exchange(contrib, 1)
-    neumann_piece = jnp.sum(local_inverse * restricted[None, :, :], axis=1)
-    sent = call(
-        functools.partial(correct_kernel, span=span),
-        message,
-        neumann_piece,
-        contribs,
-        coarse_inverse,
+    anywhere, here = pl.BlockSpec(memory_space=pltpu.HBM), pl.BlockSpec(memory_space=pltpu.VMEM)
+    requests, ids = call(
+        plan_kernel,
+        (shape((devices, LANES), jnp.int32), shape((2, slots), jnp.int32)),
         owner,
-        rank,
+        row,
+        in_specs=[anywhere] * 2,
+        scratch_shapes=[
+            pltpu.VMEM((1, slots), jnp.int32),
+            pltpu.VMEM((1, slots), jnp.int32),
+            pltpu.SemaphoreType.DMA((2,)),
+        ],
+    )
+    weight, chosen, vectors, coarse, named, gram, last = call(
+        prepare_kernel,
+        (
+            shape((1, slots), F32),
+            shape((nprim, slots), F32),
+            shape((width, nprim), F32),
+            shape((PAIRS * nprim, LANES), F32),
+            shape((devices, nprim), BF16),
+            shape((32, LANES), F32),
+            shape((width, rows), F32),
+        ),
+        ids,
         weight,
         prim,
         prim_vector,
+        basis,
+    )
+    arrived = exchange(requests, 1)
+    asked, sent = call(
+        fetch_kernel,
+        (shape((2 * PAIRS, devices), jnp.int32), message),
+        arrived,
+        last,
+    )
+    restricted, contrib = call(
+        restrict_kernel, (field, square), exchange(sent, PAIRS), ids, weight, chosen, vectors
+    )
+    contribs = exchange(contrib, 1)
+    packed = call(
+        neumann_kernel,
+        message,
+        local_inverse,
+        restricted,
+        ids,
+        weight,
+        vmem=50,
+        in_specs=[anywhere, here, here, here],
+        scratch_shapes=[
+            pltpu.VMEM((width, slots), F32),
+            pltpu.VMEM(local_inverse.shape, BF16),
+            pltpu.SemaphoreType.DMA((slots // LANES,)),
+        ],
+    )
+    sent = call(
+        functools.partial(correct_kernel, span=span), message, packed, contribs, coarse_inverse, coarse, named
     )
     sent = call(functools.partial(assemble_kernel, rows=rows), message, exchange(sent, PAIRS), asked)
-    restored, gathered = call(
-        restore_kernel,
-        (field, shape((kc, width, inner), F32)),
+    sent = call(
+        schur_kernel,
+        message,
         exchange(sent, PAIRS),
-        owner,
-        rank,
+        ids,
         coupling_index,
-    )
-    interior_in = jnp.sum(coupling_blocks * gathered[:, None, :, :], axis=(0, 2))
-    interior_sol = jnp.sum(interior_inverse * interior_in[None, :, :], axis=1)
-    backward = jnp.sum(coupling_blocks * interior_sol[None, :, None, :], axis=1)
-    sent = call(
-        image_kernel,
-        message,
-        backward,
-        restored,
         interface_shifted_diagonal,
-        owner,
-        rank,
-        coupling_index,
+        coupling_blocks,
+        interior_inverse,
+        vmem=50,
+        in_specs=[here] * 4 + [anywhere] * 2,
+        scratch_shapes=[
+            pltpu.VMEM((kc, width, inner), F32),
+            pltpu.VMEM((width, inner), F32),
+            pltpu.VMEM((kc, width, inner), F32),
+            pltpu.VMEM(coupling_blocks.shape, BF16),
+            pltpu.VMEM(interior_inverse.shape, BF16),
+            pltpu.SemaphoreType.DMA((inner // LANES, 2)),
+        ],
     )
     image, stats = call(
-        final_kernel, (shape((width, rows), F32), square), exchange(sent, PAIRS), asked, basis
+        final_kernel,
+        (shape((width, rows), F32), square),
+        exchange(sent, PAIRS),
+        asked,
+        basis,
+        gram,
+        scratch_shapes=[pltpu.VMEM((16, LANES), F32)],
     )
     direction, coeffs = call(
         functools.partial(finish_kernel, entries=entries),

time: 150 us -> 143 us (0.953)
  blocking collectives: 68.3 us -> 86.1 us
  waiting for transfers between devices: 25.3 us -> 9.69 us
  other arithmetic: 15.2 us -> 0 us
  Pallas kernels: 14.5 us -> 25.3 us
  starting transfers between devices: 19.1 us -> 15.1 us
    all_to_all x4 -> x5, blocking collectives: 68.3 us -> 86.1 us  [exchange(): lax.all_to_all(sent, ('stream', 'span'), split_axis=0, concat_axis=0, til...]
    all_to_all x3 -> x2, waiting for transfers between devices: 25.3 us -> 9.69 us  [exchange(): lax.all_to_all(sent, ('stream', 'span'), split_axis=0, concat_axis=0, til...]
    reduce_sum x4 -> x0, other arithmetic: 15.2 us -> none  [the longest x1 6.16 us: body(): neumann_piece = jnp.sum(local_inverse * restricted[None, :, :], axis=1)]
    pallas_call x9 -> x10, Pallas kernels: 14.5 us -> 25.3 us  [call(): pl.pallas_call(kernel, out_shape=out_shape, compiler_params=pltpu.Compile...]
    all_to_all x3 -> x2, starting transfers between devices: 19.1 us -> 15.1 us  [exchange(): lax.all_to_all(sent, ('stream', 'span'), split_axis=0, concat_axis=0, til...]
    unnamed x27 -> x17, local copies, waits for them, and re-layouts: 3.62 us -> 3.94 us
  transfers between devices with their start and end apart: 3 -> 2, of which waited for: 3 -> 2; matrix products, arithmetic and copies ran while one was open for 6% -> 1% of each run, Pallas kernels for 0% -> 5%
where the time goes in v1:
time: 143 us; the launch traced here: 142 us
  blocking collectives  86.1 us (60%)
  Pallas kernels  25.3 us (18%)
  starting transfers between devices  15.1 us (11%)
  waiting for transfers between devices  9.69 us (7%)
  local copies, waits for them, and re-layouts  5.19 us (4%)
    all_to_all x5, blocking collectives, exchange(): lax.all_to_all(sent, ('stream', 'span'), split_axis=0, concat_axis=0, til...  86.1 us
    pallas_call x10, Pallas kernels, call(): pl.pallas_call(kernel, out_shape=out_shape, compiler_params=pltpu.Compile...  25.3 us
    all_to_all x2, starting transfers between devices, exchange(): lax.all_to_all(sent, ('stream', 'span'), split_axis=0, concat_axis=0, til...  15.1 us
    all_to_all x2, waiting for transfers between devices, exchange(): lax.all_to_all(sent, ('stream', 'span'), split_axis=0, concat_axis=0, til...  9.69 us
    unnamed x17, local copies, waits for them, and re-layouts  3.94 us
  transfers between devices with their start and end apart: 2, of which 2 were waited for; matrix products, arithmetic and copies ran while one was open for 1% of the time, Pallas kernels for 5%

profile of v1, /device:TPU:1, one launch (start us, length us, event | category | flops | bytes accessed | tf_op | source)
XLA Modules:
  0.0 142.2 jit_solution(3377407794448528767)
XLA Ops:
  0.6 0.0 copy-start.3
  0.6 0.0 copy-start.5
  0.7 0.0 copy-start.6
  0.7 0.7 copy-done.6
  1.4 0.7 copy-done.7
  2.1 1.2 shard_map.131
  3.2 11.5 %all-to-all-start = ((s32[128,1,128]{2,1,0:T(1,128)}), s32[128,1,128]{2,1,0:T(1,128)S(1)}, u32[]{:S(2)}, u32[]{:S(2)}) async-start(s32[128,1,128]{2,1,0:T(1,128)} %bitcast.3), calls=%async_computation | async-start | bytes 131072 | tf_op jit(solution)/shard_map/all_to_all | solution.py:489
  14.8 0.7 copy.17.prim_ref
  15.5 0.8 copy.18.vector_ref
  16.3 1.0 copy-done
  17.3 0.7 copy-done.4
  18.0 1.0 shard_map.132
  19.0 5.6 %all-to-all-done = s32[128,1,128]{2,1,0:T(1,128)S(1)} async-done(((s32[128,1,128]{2,1,0:T(1,128)}), s32[128,1,128]{2,1,0:T(1,128)S(1)}, u32[]{:S(2)}, u32[]{:S(2)}) %all-to-all-start) | async-done | bytes 65568 | tf_op jit(solution)/shard_map/all_to_all | solution.py:489
  24.6 0.6 shard_map.133
  25.2 18.2 %all_to_all.35 = f32[128,8,128]{2,1,0:T(8,128)S(1)} all-to-all(f32[128,8,128]{2,1,0:T(8,128)S(1)} %bitcast.33), channel_id=1, replica_groups=mesh['stream'=32,'span'=4] {'stream','span'}, dimensions={0} | all-to-all | bytes 1048576 | tf_op jit(solution)/shard_map/all_to_all | solution.py:489
  43.3 1.8 %shard_map.134 = (f32[64,1024]{1,0:T(8,128)S(1)}, f32[128,128]{1,0:T(8,128)}) custom-call(f32[1024,128]{1,0:T(8,128)S(1)} %bitcast.29, s32[2,1024]{1,0:T(2,128)S(1)} %get-tuple-element.20.ids_ref, f32[1,1024]{1,0:T(1,128)S(1)} %get-tuple-element.23.weight_ref, f32[32,1024]{1,0:T(8,128)S(1)} %get-tuple-element.24.chosen_ref, ...), custom_call_target="tpu_custom_call" | custom-call | tf_op jit(solution)/shard_map/pallas_call | solution.py:40
  45.2 3.6 %all-to-all-start.2 = ((f32[128,1,128]{2,1,0:T(1,128)}), f32[128,1,128]{2,1,0:T(1,128)S(1)}, u32[]{:S(2)}, u32[]{:S(2)}) async-start(f32[128,1,128]{2,1,0:T(1,128)} %bitcast.10), calls=%async_computation.2 | async-start | bytes 131072 | tf_op jit(solution)/shard_map/all_to_all | solution.py:489
  48.8 5.8 %shard_map.135.packed_ref = f32[1024,128]{1,0:T(8,128)S(1)} custom-call(bf16[64,64,1024]{2,1,0:T(8,128)(2,1)} %blocks_hbm.1, f32[64,1024]{1,0:T(8,128)S(1)} %get-tuple-element.26.restricted_ref, s32[2,1024]{1,0:T(2,128)S(1)} %get-tuple-element.20.ids_ref, f32[1,1024]{1,0:T(1,128)S(1)} %get-tuple-element.23.weight_ref), custom_call_target="tpu_custom_call" | custom-call | tf_op jit(solution)/shard_map/pallas_call | solution.py:40
  54.6 4.1 %all-to-all-done.2 = f32[128,1,128]{2,1,0:T(1,128)S(1)} async-done(((f32[128,1,128]{2,1,0:T(1,128)}), f32[128,1,128]{2,1,0:T(1,128)S(1)}, u32[]{:S(2)}, u32[]{:S(2)}) %all-to-all-start.2) | async-done | bytes 65568 | tf_op jit(solution)/shard_map/all_to_all | solution.py:489
  58.8 0.0 copy-done.3
  58.8 0.9 shard_map.136
  59.7 19.7 %all_to_all.36 = f32[128,8,128]{2,1,0:T(8,128)S(1)} all-to-all(f32[128,8,128]{2,1,0:T(8,128)S(1)} %bitcast.32), channel_id=1, replica_groups=mesh['stream'=32,'span'=4] {'stream','span'}, dimensions={0} | all-to-all | bytes 1048576 | tf_op jit(solution)/shard_map/all_to_all | solution.py:489
  79.4 1.3 shard_map.137
  80.8 17.5 %all_to_all.37 = f32[128,8,128]{2,1,0:T(8,128)S(1)} all-to-all(f32[128,8,128]{2,1,0:T(8,128)S(1)} %bitcast.31), channel_id=1, replica_groups=mesh['stream'=32,'span'=4] {'stream','span'}, dimensions={0} | all-to-all | bytes 1048576 | tf_op jit(solution)/shard_map/all_to_all | solution.py:489
  98.3 0.0 copy-done.5
  98.3 0.0 copy-done.2
  98.3 10.2 %shard_map.138 = f32[1024,128]{1,0:T(8,128)S(1)} custom-call(f32[1024,128]{1,0:T(8,128)S(1)} %bitcast.26, s32[2,1024]{1,0:T(2,128)S(1)} %get-tuple-element.20.ids_ref, s32[2,512]{1,0:T(2,128)S(1)} %copy-done.5, f32[64,1024]{1,0:T(8,128)S(1)} %copy-done.2, bf16[2,64,64,512]{3,2,1,0:T(8,128)(2,1)} %coupling_hbm.1, bf16[64,64,512]{2,1,0:T(8,128)(2,1)} %inverse_hbm.1), custom_call_target="tpu_custom_call" | custom-call | tf_op jit(solution)/shard_map/pallas_call | solution.py:40
  108.4 17.5 %all_to_all.38 = f32[128,8,128]{2,1,0:T(8,128)S(1)} all-to-all(f32[128,8,128]{2,1,0:T(8,128)S(1)} %bitcast.27), channel_id=1, replica_groups=mesh['stream'=32,'span'=4] {'stream','span'}, dimensions={0} | all-to-all | bytes 1048576 | tf_op jit(solution)/shard_map/all_to_all | solution.py:489
  125.9 1.5 %shard_map.139 = (f32[64,512]{1,0:T(8,128)S(1)}, f32[128,128]{1,0:T(8,128)S(1)}) custom-call(f32[1024,128]{1,0:T(8,128)S(1)} %bitcast.28, s32[16,128]{1,0:T(8,128)S(1)} %get-tuple-element.30.asked_ref, f32[4,64,512]{2,1,0:T(8,128)S(1)} %copy-done.1, f32[32,128]{1,0:T(8,128)S(1)} %get-tuple-element.31.gram_ref), custom_call_target="tpu_custom_call" | custom-call | tf_op jit(solution)/shard_map/pallas_call | solution.py:40
  127.4 13.2 %all_to_all.39 = f32[128,1,128]{2,1,0:T(1,128)S(1)} all-to-all(f32[128,1,128]{2,1,0:T(1,128)S(1)} %bitcast.37), channel_id=1, replica_groups=mesh['stream'=32,'span'=4] {'stream','span'}, dimensions={0} | all-to-all | bytes 131072 | tf_op jit(solution)/shard_map/all_to_all | solution.py:489
  140.7 1.0 shard_map.140
  141.7 0.5 slice_bitcast_fusion
  (6 shorter events, 0.0 us)
Async XLA Ops:
  0.6 58.1 %copy-start.3 = (f32[32,1024]{1,0:T(8,128)S(1)}, f32[32,1024]{1,0:T(8,128)}, u32[]{:S(2)}) copy-start(f32[32,1024]{1,0:T(8,128)} %inverse_ref.1) | copy-start | bytes 393220
  0.6 97.6 %copy-start.5 = (s32[2,512]{1,0:T(2,128)S(1)}, s32[2,512]{1,0:T(2,128)}, u32[]{:S(2)}) copy-start(s32[2,512]{1,0:T(2,128)} %index_ref.1) | copy-start | bytes 12292
  0.7 0.7 copy-start.6
  1.4 0.7 copy-start.7
  3.2 21.3 %all-to-all-start = ((s32[128,1,128]{2,1,0:T(1,128)}), s32[128,1,128]{2,1,0:T(1,128)S(1)}, u32[]{:S(2)}, u32[]{:S(2)}) async-start(s32[128,1,128]{2,1,0:T(1,128)} %bitcast.3), calls=%async_computation | async-start | bytes 131072 | tf_op jit(solution)/shard_map/all_to_all | solution.py:489
  16.3 1.0 copy-start
  17.3 0.7 copy-start.4
  18.0 80.2 %copy-start.2 = (f32[64,1024]{1,0:T(8,128)S(1)}, f32[64,1024]{1,0:T(8,128)}, u32[]{:S(2)}) copy-start(f32[64,1024]{1,0:T(8,128)} %diagonal_ref.1) | copy-start | bytes 786436
  45.2 13.6 %all-to-all-start.2 = ((f32[128,1,128]{2,1,0:T(1,128)}), f32[128,1,128]{2,1,0:T(1,128)S(1)}, u32[]{:S(2)}, u32[]{:S(2)}) async-start(f32[128,1,128]{2,1,0:T(1,128)} %bitcast.10), calls=%async_computation.2 | async-start | bytes 131072 | tf_op jit(solution)/shard_map/all_to_all | solution.py:489
  79.4 46.5 %copy-start.1 = (f32[4,64,512]{2,1,0:T(8,128)S(1)}, f32[4,64,512]{2,1,0:T(8,128)}, u32[]{:S(2)}) copy-start(f32[4,64,512]{2,1,0:T(8,128)} %basis_ref.5) | copy-start | bytes 1572868

commit v2 on v1

--- a/solution.py
+++ b/solution.py
@@ -36,7 +36,9 @@
     return pl.ds(k, count, stride=PAIRS)
 
 
-def call(kernel, out_shape, *args, vmem=16, **kw):
+def call(kernel, out_shape, *args, vmem=16, flops=0, **kw):
+    if flops:
+        kw["cost_estimate"] = pl.CostEstimate(flops=flops, bytes_accessed=flops // 100, transcendentals=0)
     return pl.pallas_call(
         kernel,
         out_shape=out_shape,
@@ -45,19 +47,12 @@
     )(*args)
 
 
-def plan_kernel(owner_hbm, row_hbm, request_ref, ids_ref, owner_ref, row_ref, sems):
-    slots = owner_ref.shape[1]
+def plan_kernel(row_of_ref, request_ref, ids_ref, *, rows):
+    slots = row_of_ref.shape[1]
     devices = request_ref.shape[0]
-    copies = [
-        pltpu.make_async_copy(owner_hbm, owner_ref, sems.at[0]),
-        pltpu.make_async_copy(row_hbm, row_ref, sems.at[1]),
-    ]
-    for copy in copies:
-        copy.start()
-    for copy in copies:
-        copy.wait()
-    owner = owner_ref[...]
-    row = row_ref[...]
+    row_of = row_of_ref[...]
+    owner = lax.div(row_of, rows)
+    row = row_of - owner * rows
     named = one_hot(lax.broadcasted_iota(jnp.int32, (devices, slots), 0) == owner)
     before = lax.broadcasted_iota(jnp.int32, (LANES, LANES), 0) < lax.broadcasted_iota(
         jnp.int32, (LANES, LANES), 1
@@ -106,13 +101,13 @@
 def slots_to_messages(values, owner, rank, message_ref):
     slots = owner.shape[1]
     devices = message_ref.shape[0] // PAIRS
-    high, low = split(values)
+    first = (rank & 1) == 0
+    sides = jnp.concatenate([jnp.where(first, values, 0.0), jnp.where(first, 0.0, values)], axis=0).T
+    sides = jnp.concatenate(split(sides), axis=1)
     named = one_hot(lax.broadcasted_iota(jnp.int32, (devices, slots), 0) == owner)
+    pair = rank >> 1
     for k in range(PAIRS):
-        first = one_hot(rank == 2 * k)
-        second = one_hot(rank == 2 * k + 1)
-        placed = jnp.concatenate([high * first, high * second, low * first, low * second], axis=0)
-        both = mm_nt(named, placed)
+        both = mm(named * one_hot(pair == k), sides)
         message_ref[message_rows(k, devices), :] = both[:, :LANES] + both[:, LANES:]
 
 
@@ -127,21 +122,28 @@
     return total
 
 
+def row_tile(block_refs, vectors, first, lanes):
+    row = lax.broadcasted_iota(jnp.int32, (8, LANES), 0)
+    result = jnp.zeros((8, LANES), F32)
+    for j in range(8):
+        result = jnp.where(row == j, block_sums(block_refs, vectors, first + j, lanes), result)
+    return result
+
+
 def apply_blocks(block_refs, vector_refs, out_ref, c):
-    width = out_ref.shape[0]
-    row = lax.broadcasted_iota(jnp.int32, (8, LANES), 0)
     lanes = slice(c * LANES, (c + 1) * LANES)
     vectors = [ref[:, lanes] for ref in vector_refs]
 
     def rows_of(tile, _):
         first = pl.multiple_of(tile * 8, 8)
-        result = jnp.zeros((8, LANES), F32)
-        for j in range(8):
-            result = jnp.where(row == j, block_sums(block_refs, vectors, first + j, lanes), result)
-        out_ref[pl.ds(first, 8), lanes] = result
+        out_ref[pl.ds(first, 8), lanes] = row_tile(block_refs, vectors, first, lanes)
         return 0
 
-    lax.fori_loop(0, width // 8, rows_of, 0)
+    lax.fori_loop(0, out_ref.shape[0] // 8, rows_of, 0)
+
+
+def as_column(row):
+    return jnp.broadcast_to(row.astype(F32), (8, row.shape[1])).T[:, :1]
 
 
 def prepare_kernel(
@@ -159,11 +161,12 @@
     last_ref,
 ):
     slots = ids_ref.shape[1]
-    nprim = prim_ref.shape[0]
+    nprim = vector_ref.shape[0]
     devices = named_ref.shape[0]
-    chosen = lax.broadcasted_iota(jnp.int32, (nprim, slots), 1) == prim_ref[...]
+    prim = as_column(prim_ref[...])[:nprim].astype(jnp.int32)
+    chosen = lax.broadcasted_iota(jnp.int32, (nprim, slots), 1) == prim
     weights_ref[...] = weight_ref[...]
-    chosen_ref[...] = jnp.where(chosen, 1.0, 0.0)
+    chosen_ref[...] = one_hot(chosen)
     vectors_ref[...] = vector_ref[...]
 
     def column(values):
@@ -173,7 +176,7 @@
     named_ref[...] = one_hot(
         lax.broadcasted_iota(jnp.int32, (nprim, devices), 1).astype(F32) == owner
     ).astype(F32).T.astype(BF16)
-    vectors = vector_ref[...].T * weight
+    vectors = vector_ref[...] * weight
     for k in range(PAIRS):
         sides = [jnp.where(rank == 2.0 * k + side, vectors, 0.0) for side in range(2)]
         coarse_ref[k * nprim : (k + 1) * nprim, :] = jnp.concatenate(sides, axis=1)
@@ -183,26 +186,35 @@
     store_sums([(fields[i], fields[j]) for i in range(kb) for j in range(i, kb)], gram_ref)
 
 
-def restrict_kernel(message_ref, ids_ref, weight_ref, chosen_ref, vector_ref, out_ref, contrib_ref):
+def restrict_kernel(
+    message_ref, ids_ref, weight_ref, chosen_ref, vector_ref, out_ref, contrib_ref
+):
     restricted = slots_from_messages(message_ref, ids_ref[0:1, :], ids_ref[1:2, :]) * weight_ref[...]
     out_ref[...] = restricted
-    at_prim = mm_nt(restricted, chosen_ref[...], HIGH)
-    contrib = jnp.sum(at_prim * vector_ref[...], axis=0, keepdims=True)
-    wide = jnp.concatenate([contrib, jnp.zeros((1, LANES - contrib.shape[1]), F32)], axis=1)
-    contrib_ref[...] = jnp.broadcast_to(wide, contrib_ref.shape)
+    nprim = chosen_ref.shape[0]
+    at_prim = sum(mm_nt(chosen_ref[...], part) for part in split(restricted))
+    contrib = jnp.sum(at_prim * vector_ref[...], axis=1, keepdims=True)
+    square = jnp.broadcast_to(contrib, (nprim, contrib_ref.shape[0])).T
+    contrib_ref[...] = jnp.concatenate([square, jnp.zeros((square.shape[0], LANES - nprim), F32)], axis=1)
 
 
 def neumann_kernel(blocks_hbm, restricted_ref, ids_ref, weight_ref, message_ref, piece_ref, blocks_ref, sems):
-    columns = piece_ref.shape[1]
+    width, slots = piece_ref.shape
     copies = []
-    for c in range(columns // LANES):
-        lanes = pl.ds(c * LANES, LANES)
-        copies.append(pltpu.make_async_copy(blocks_hbm.at[:, :, lanes], blocks_ref.at[:, :, lanes], sems.at[c]))
+    for n in range(width // 8):
+        rows = pl.ds(n * 8, 8)
+        copies.append(pltpu.make_async_copy(blocks_hbm.at[rows], blocks_ref.at[rows], sems.at[n]))
     for copy in copies:
         copy.start()
-    for c, copy in enumerate(copies):
+    for n, copy in enumerate(copies):
         copy.wait()
-        apply_blocks([blocks_ref], [restricted_ref], piece_ref, c)
+
+        def chunk(c, _, first=n * 8):
+            lanes = pl.ds(pl.multiple_of(c * LANES, LANES), LANES)
+            piece_ref[first : first + 8, lanes] = row_tile([blocks_ref], [restricted_ref[:, lanes]], first, lanes)
+            return 0
+
+        lax.fori_loop(0, slots // LANES, chunk, 0)
     slots_to_messages(piece_ref[...] * weight_ref[...], ids_ref[0:1, :], ids_ref[1:2, :], message_ref)
 
 
@@ -230,29 +242,15 @@
     ids_ref,
     index_ref,
     diagonal_ref,
-    coupling_hbm,
-    inverse_hbm,
+    coupling_ref,
+    inverse_ref,
     message_ref,
     gathered_ref,
     inner_ref,
     backward_ref,
-    coupling_ref,
-    inverse_ref,
-    sems,
 ):
     kc, inner = index_ref.shape
     chunks = inner // LANES
-    copies = []
-    for c in range(chunks):
-        lanes = pl.ds(c * LANES, LANES)
-        copies.append(
-            pltpu.make_async_copy(coupling_hbm.at[:, :, :, lanes], coupling_ref.at[:, :, :, lanes], sems.at[c, 0])
-        )
-        copies.append(
-            pltpu.make_async_copy(inverse_hbm.at[:, :, lanes], inverse_ref.at[:, :, lanes], sems.at[c, 1])
-        )
-    for copy in copies:
-        copy.start()
     owner, rank = ids_ref[0:1, :], ids_ref[1:2, :]
     restored = slots_from_messages(arrived_ref, owner, rank)
     width, slots = restored.shape
@@ -263,8 +261,6 @@
         gathered_ref[k] = got[:width] + got[width:]
     blocks = [coupling_ref.at[k] for k in range(kc)]
     for c in range(chunks):
-        for copy in copies[2 * c : 2 * c + 2]:
-            copy.wait()
         apply_blocks(blocks, [gathered_ref.at[k] for k in range(kc)], inner_ref, c)
         lanes = slice(c * LANES, (c + 1) * LANES)
         vector = inner_ref[:, lanes]
@@ -286,8 +282,9 @@
     value = diagonal_ref[...] * restored
     for k in range(kc):
         both = jnp.concatenate(split(backward_ref[k]), axis=0)
-        chosen = one_hot(lax.broadcasted_iota(jnp.int32, (slots, inner), 0) == index_ref[k : k + 1, :])
-        got = mm_nt(both, chosen)
+        index = as_column(index_ref[k : k + 1, :]).astype(jnp.int32)
+        chosen = one_hot(lax.broadcasted_iota(jnp.int32, (inner, slots), 1) == index)
+        got = mm(both, chosen)
         value = value - (got[:width] + got[width:])
     slots_to_messages(value, owner, rank, message_ref)
 
@@ -350,6 +347,16 @@
 def pair_add(a, b):
     total, rest = two_sum(a[0], b[0])
     return total, rest + (a[1] + b[1])
+
+
+def two_product(a, b):
+    a_high = a * 4097.0
+    a_high = a_high - (a_high - a)
+    b_high = b * 4097.0
+    b_high = b_high - (b_high - b)
+    a_low, b_low = a - a_high, b - b_high
+    product = a * b
+    return product, ((a_high * b_high - product) + a_high * b_low + a_low * b_high) + a_low * b_low
 
 
 def store_sums(products, out_ref):
@@ -408,50 +415,35 @@
         )
         half //= 2
     lane = lax.broadcasted_iota(jnp.int32, (1, LANES), 1)
-
-    def entry(n):
-        return tuple(jnp.sum(jnp.where(lane == n, p, 0.0), axis=1, keepdims=True) for p in pair)
-
-    numbers = [entry(n) for n in range(1 + kb)]
-    numbers += [entry(gram + n) for n in range(kb * (kb + 1) // 2)]
     inv_root = 1.0 / math.sqrt(entries)
-    projected = [(numbers[1 + k][0] + numbers[1 + k][1]) * inv_root for k in range(kb)]
-    steps = [p * inv_root for p in projected]
-
-    def add_product(total, factor, number):
-        a, b = factor, number[0]
-        a_high = a * 4097.0
-        a_high = a_high - (a_high - a)
-        b_high = b * 4097.0
-        b_high = b_high - (b_high - b)
-        a_low, b_low = a - a_high, b - b_high
-        product = a * b
-        rest = ((a_high * b_high - product) + a_high * b_low + a_low * b_high) + a_low * b_low
-        return pair_add(total, (product, rest + factor * number[1]))
-
-    def scaled(number, factor):
-        zero = jnp.zeros_like(factor)
-        return add_product((zero, zero), factor, number)
-
-    total = numbers[0]
-    at = 1 + kb
+    projected = (pair[0] + pair[1]) * inv_root
+    steps = [
+        jnp.sum(jnp.where(lane == 1 + k, projected, 0.0), axis=1, keepdims=True) * inv_root for k in range(kb)
+    ]
+    left = jnp.where(lane == 0, 1.0, 0.0)
+    right = jnp.ones((1, LANES), F32)
+    at = gram
     for k in range(kb):
-        total = add_product(total, -2.0 * steps[k], numbers[1 + k])
-    for k in range(kb):
+        left = jnp.where(lane == 1 + k, -2.0 * steps[k], left)
         for other in range(k, kb):
-            factor = steps[k] if other == k else 2.0 * steps[k]
-            total = add_product(total, factor, scaled(numbers[at], steps[other]))
+            left = jnp.where(lane == at, steps[k] if other == k else 2.0 * steps[k], left)
+            right = jnp.where(lane == at, steps[other], right)
             at += 1
-    squares = jnp.maximum(total[0] + total[1], 0.0)
+    factor, factor_rest = two_product(left, right)
+    total, rest = two_product(factor, pair[0])
+    pair = (total, rest + (factor * pair[1] + factor_rest * pair[0]))
+    shift = gram
+    while shift:
+        pair = pair_add(pair, tuple(pltpu.roll(p, LANES - shift, 1) for p in pair))
+        shift //= 2
+    squares = jnp.maximum((pair[0] + pair[1])[:, :1], 0.0)
     root_mean = jnp.sqrt(squares / entries + 1e-06)
     remainder = image_ref[...]
     for k in range(kb):
         remainder = remainder - steps[k] * basis_ref[k]
     direction_ref[...] = remainder / root_mean
-    coeffs = jnp.zeros((1, LANES), F32)
-    for n, value in enumerate(projected + [root_mean]):
-        coeffs = jnp.where(lane == n, value, coeffs)
-    coeff_ref[...] = coeffs
+    values = jnp.where(lane == kb, root_mean, pltpu.roll(projected, LANES - 1, 1))
+    coeff_ref[...] = values[0, : kb + 1]
 
 
 def body(
@@ -478,7 +470,7 @@
     owner = interface_row_owner.reshape(1, slots)
     row = interface_local_row.reshape(1, slots)
     weight = interface_slot_weight.reshape(1, slots)
-    prim = prim_index.reshape(nprim, 1)
+    prim = prim_index.reshape(1, nprim)
     shape = jax.ShapeDtypeStruct
     message = shape((devices * PAIRS, LANES), F32)
     field = shape((width, slots), F32)
@@ -488,25 +480,18 @@
         sent = x.reshape(devices, per, LANES)
         return lax.all_to_all(sent, ("stream", "span"), split_axis=0, concat_axis=0, tiled=True).reshape(x.shape)
 
-    anywhere, here = pl.BlockSpec(memory_space=pltpu.HBM), pl.BlockSpec(memory_space=pltpu.VMEM)
     requests, ids = call(
-        plan_kernel,
+        functools.partial(plan_kernel, rows=rows),
         (shape((devices, LANES), jnp.int32), shape((2, slots), jnp.int32)),
-        owner,
-        row,
-        in_specs=[anywhere] * 2,
-        scratch_shapes=[
-            pltpu.VMEM((1, slots), jnp.int32),
-            pltpu.VMEM((1, slots), jnp.int32),
-            pltpu.SemaphoreType.DMA((2,)),
-        ],
+        owner * rows + row,
+        flops=20_000_000_000,
     )
     weight, chosen, vectors, coarse, named, gram, last = call(
         prepare_kernel,
         (
             shape((1, slots), F32),
-            shape((nprim, slots), F32),
-            shape((width, nprim), F32),
+            shape((nprim, slots), BF16),
+            shape((nprim, width), F32),
             shape((PAIRS * nprim, LANES), F32),
             shape((devices, nprim), BF16),
             shape((32, LANES), F32),
@@ -515,16 +500,12 @@
         ids,
         weight,
         prim,
-        prim_vector,
+        prim_vector.T,
         basis,
     )
     arrived = exchange(requests, 1)
-    asked, sent = call(
-        fetch_kernel,
-        (shape((2 * PAIRS, devices), jnp.int32), message),
-        arrived,
-        last,
-    )
+    asked, sent = call(fetch_kernel, (shape((2 * PAIRS, devices), jnp.int32), message), arrived, last)
+    anywhere, here = pl.BlockSpec(memory_space=pl.ANY), pl.BlockSpec(memory_space=pltpu.VMEM)
     restricted, contrib = call(
         restrict_kernel, (field, square), exchange(sent, PAIRS), ids, weight, chosen, vectors
     )
@@ -541,13 +522,19 @@
         scratch_shapes=[
             pltpu.VMEM((width, slots), F32),
             pltpu.VMEM(local_inverse.shape, BF16),
-            pltpu.SemaphoreType.DMA((slots // LANES,)),
+            pltpu.SemaphoreType.DMA((width // 8,)),
         ],
     )
     sent = call(
         functools.partial(correct_kernel, span=span), message, packed, contribs, coarse_inverse, coarse, named
     )
-    sent = call(functools.partial(assemble_kernel, rows=rows), message, exchange(sent, PAIRS), asked)
+    sent = call(
+        functools.partial(assemble_kernel, rows=rows),
+        message,
+        exchange(sent, PAIRS),
+        asked,
+        flops=20_000_000_000,
+    )
     sent = call(
         schur_kernel,
         message,
@@ -557,15 +544,10 @@
         interface_shifted_diagonal,
         coupling_blocks,
         interior_inverse,
-        vmem=50,
-        in_specs=[here] * 4 + [anywhere] * 2,
         scratch_shapes=[
             pltpu.VMEM((kc, width, inner), F32),
             pltpu.VMEM((width, inner), F32),
             pltpu.VMEM((kc, width, inner), F32),
-            pltpu.VMEM(coupling_blocks.shape, BF16),
-            pltpu.VMEM(interior_inverse.shape, BF16),
-            pltpu.SemaphoreType.DMA((inner // LANES, 2)),
         ],
     )
     image, stats = call(
@@ -577,14 +559,13 @@
         gram,
         scratch_shapes=[pltpu.VMEM((16, LANES), F32)],
     )
-    direction, coeffs = call(
+    return call(
         functools.partial(finish_kernel, entries=entries),
-        (shape((width, rows), F32), shape((1, LANES), F32)),
+        (shape((width, rows), F32), shape((kb + 1,), F32)),
         exchange(stats, 1),
         image,
         basis,
     )
-    return direction, coeffs[0, : kb + 1]
 
 
 def solution(mesh):

time: 143 us -> 140 us (0.979)
  local copies, waits for them, and re-layouts: 5.19 us -> 0.04 us
  waiting for transfers between devices: 9.69 us -> 13.2 us
  Pallas kernels: 25.3 us -> 23.5 us
    unnamed x17 -> x20, local copies, waits for them, and re-layouts: 3.94 us -> 0.04 us
    all_to_all x2, waiting for transfers between devices: 9.69 us -> 13.2 us  [exchange(): lax.all_to_all(sent, ('stream', 'span'), split_axis=0, concat_axis=0, til...]
    pallas_call x10, Pallas kernels: 25.3 us -> 23.5 us  [call(): pl.pallas_call(kernel, out_shape=out_shape, compiler_params=pltpu.Compile...]
  transfers between devices with their start and end apart: 2 -> 2, of which waited for: 2 -> 2; matrix products, arithmetic and copies ran while one was open for 1% -> 0% of each run, Pallas kernels for 5% -> 5%
where the time goes in v2:
time: 140 us
  blocking collectives  85.6 us (61%)
  Pallas kernels  23.5 us (17%)
  starting transfers between devices  15.1 us (11%)
  waiting for transfers between devices  13.2 us (9%)
    all_to_all x5, blocking collectives, exchange(): lax.all_to_all(sent, ('stream', 'span'), split_axis=0, concat_axis=0, til...  85.6 us
    pallas_call x10, Pallas kernels, call(): pl.pallas_call(kernel, out_shape=out_shape, compiler_params=pltpu.Compile...  23.5 us
    all_to_all x2, starting transfers between devices, exchange(): lax.all_to_all(sent, ('stream', 'span'), split_axis=0, concat_axis=0, til...  15.1 us
    all_to_all x2, waiting for transfers between devices, exchange(): lax.all_to_all(sent, ('stream', 'span'), split_axis=0, concat_axis=0, til...  13.2 us
  transfers between devices with their start and end apart: 2, of which 2 were waited for; matrix products, arithmetic and copies ran while one was open for 0% of the time, Pallas kernels for 5%

profile of v2, /device:TPU:1, one launch (start us, length us, event | category | flops | bytes accessed | tf_op | source)
XLA Modules:
  0.0 139.6 jit_solution(5689128086982780413)
XLA Ops:
  0.6 0.7 broadcast_multiply_fusion
  1.3 0.7 add.5
  2.0 0.0 copy-start
  2.0 1.2 shard_map.131
  3.2 11.5 %all-to-all-start = ((s32[128,1,128]{2,1,0:T(1,128)}), s32[128,1,128]{2,1,0:T(1,128)S(1)}, u32[]{:S(2)}, u32[]{:S(2)}) async-start(s32[128,1,128]{2,1,0:T(1,128)} %bitcast.3), calls=%async_computation | async-start | bytes 131072 | tf_op jit(solution)/shard_map/all_to_all | solution.py:481
  14.7 0.0 copy-done
  14.7 0.0 copy-done.4
  14.7 0.0 copy-done.5
  14.7 0.0 copy-done.7
  14.7 1.1 shard_map.132
  15.8 8.7 %all-to-all-done = s32[128,1,128]{2,1,0:T(1,128)S(1)} async-done(((s32[128,1,128]{2,1,0:T(1,128)}), s32[128,1,128]{2,1,0:T(1,128)S(1)}, u32[]{:S(2)}, u32[]{:S(2)}) %all-to-all-start) | async-done | bytes 65568 | tf_op jit(solution)/shard_map/all_to_all | solution.py:481
  24.5 0.6 shard_map.133
  25.1 17.9 %all_to_all.35 = f32[128,8,128]{2,1,0:T(8,128)S(1)} all-to-all(f32[128,8,128]{2,1,0:T(8,128)S(1)} %bitcast.32), channel_id=1, replica_groups=mesh['stream'=32,'span'=4] {'stream','span'}, dimensions={0} | all-to-all | bytes 1048576 | tf_op jit(solution)/shard_map/all_to_all | solution.py:481
  43.0 1.8 %shard_map.134 = (f32[64,1024]{1,0:T(8,128)S(1)}, f32[128,128]{1,0:T(8,128)}) custom-call(f32[1024,128]{1,0:T(8,128)S(1)} %bitcast.30, s32[2,1024]{1,0:T(2,128)S(1)} %get-tuple-element.18.ids_ref, f32[1,1024]{1,0:T(1,128)S(1)} %get-tuple-element.21.weight_ref, bf16[32,1024]{1,0:T(8,128)(2,1)S(1)} %get-tuple-element.22.chosen_ref, ...), custom_call_target="tpu_custom_call" | custom-call | tf_op jit(solution)/shard_map/pallas_call | solution.py:42
  44.8 3.6 %all-to-all-start.2 = ((f32[128,1,128]{2,1,0:T(1,128)}), f32[128,1,128]{2,1,0:T(1,128)S(1)}, u32[]{:S(2)}, u32[]{:S(2)}) async-start(f32[128,1,128]{2,1,0:T(1,128)} %bitcast.11), calls=%async_computation.2 | async-start | bytes 131072 | tf_op jit(solution)/shard_map/all_to_all | solution.py:481
  48.5 5.5 %shard_map.135.packed_ref = f32[1024,128]{1,0:T(8,128)S(1)} custom-call(bf16[64,64,1024]{2,1,0:T(8,128)(2,1)} %blocks_hbm.1, f32[64,1024]{1,0:T(8,128)S(1)} %get-tuple-element.24.restricted_ref, s32[2,1024]{1,0:T(2,128)S(1)} %get-tuple-element.18.ids_ref, f32[1,1024]{1,0:T(1,128)S(1)} %get-tuple-element.21.weight_ref), custom_call_target="tpu_custom_call" | custom-call | tf_op jit(solution)/shard_map/pallas_call | solution.py:42
  54.0 4.5 %all-to-all-done.2 = f32[128,1,128]{2,1,0:T(1,128)S(1)} async-done(((f32[128,1,128]{2,1,0:T(1,128)}), f32[128,1,128]{2,1,0:T(1,128)S(1)}, u32[]{:S(2)}, u32[]{:S(2)}) %all-to-all-start.2) | async-done | bytes 65568 | tf_op jit(solution)/shard_map/all_to_all | solution.py:481
  58.4 0.0 copy-done.3
  58.5 0.9 shard_map.136
  59.4 19.4 %all_to_all.36 = f32[128,8,128]{2,1,0:T(8,128)S(1)} all-to-all(f32[128,8,128]{2,1,0:T(8,128)S(1)} %bitcast.31), channel_id=1, replica_groups=mesh['stream'=32,'span'=4] {'stream','span'}, dimensions={0} | all-to-all | bytes 1048576 | tf_op jit(solution)/shard_map/all_to_all | solution.py:481
  78.8 1.3 shard_map.137
  80.2 17.6 %all_to_all.37 = f32[128,8,128]{2,1,0:T(8,128)S(1)} all-to-all(f32[128,8,128]{2,1,0:T(8,128)S(1)} %bitcast.34), channel_id=1, replica_groups=mesh['stream'=32,'span'=4] {'stream','span'}, dimensions={0} | all-to-all | bytes 1048576 | tf_op jit(solution)/shard_map/all_to_all | solution.py:481
  97.7 0.0 slice-done
  97.7 0.0 slice-done.1
  97.7 0.0 copy-done.1
  97.7 0.0 copy-done.2
  97.7 0.0 copy-done.6
  97.8 8.3 %shard_map.138 = f32[1024,128]{1,0:T(8,128)S(1)} custom-call(f32[1024,128]{1,0:T(8,128)S(1)} %bitcast.27, s32[2,1024]{1,0:T(2,128)S(1)} %get-tuple-element.18.ids_ref, s32[2,512]{1,0:T(2,128)S(1)} %copy-done.6, f32[64,1024]{1,0:T(8,128)S(1)} %copy-done.2, bf16[2,64,64,512]{3,2,1,0:T(8,128)(2,1)S(1)} %bitcast.26, bf16[64,64,512]{2,1,0:T(8,128)(2,1)S(1)} %copy-done.1), custom_call_target="tpu_custom_call" | custom-call | tf_op jit(solution)/shard_map/pallas_call | solution.py:42
  106.1 17.5 %all_to_all.38 = f32[128,8,128]{2,1,0:T(8,128)S(1)} all-to-all(f32[128,8,128]{2,1,0:T(8,128)S(1)} %bitcast.28), channel_id=1, replica_groups=mesh['stream'=32,'span'=4] {'stream','span'}, dimensions={0} | all-to-all | bytes 1048576 | tf_op jit(solution)/shard_map/all_to_all | solution.py:481
  123.6 1.5 %shard_map.139 = (f32[64,512]{1,0:T(8,128)S(1)}, f32[128,128]{1,0:T(8,128)S(1)}) custom-call(f32[1024,128]{1,0:T(8,128)S(1)} %bitcast.29, s32[16,128]{1,0:T(8,128)S(1)} %get-tuple-element.28.asked_ref, f32[4,64,512]{2,1,0:T(8,128)S(1)} %copy-done, f32[32,128]{1,0:T(8,128)S(1)} %get-tuple-element.29.gram_ref), custom_call_target="tpu_custom_call" | custom-call | tf_op jit(solution)/shard_map/pallas_call | solution.py:42
  125.1 13.2 %all_to_all.39 = f32[128,1,128]{2,1,0:T(1,128)S(1)} all-to-all(f32[128,1,128]{2,1,0:T(1,128)S(1)} %bitcast.38), channel_id=1, replica_groups=mesh['stream'=32,'span'=4] {'stream','span'}, dimensions={0} | all-to-all | bytes 131072 | tf_op jit(solution)/shard_map/all_to_all | solution.py:481
  138.3 1.3 shard_map.140
  (10 shorter events, 0.0 us)
Async XLA Ops:
  2.0 12.7 %copy-start = (f32[4,64,512]{2,1,0:T(8,128)S(1)}, f32[4,64,512]{2,1,0:T(8,128)}, u32[]{:S(2)}) copy-start(f32[4,64,512]{2,1,0:T(8,128)} %basis_ref.5) | copy-start | bytes 1572868
  2.0 12.7 %copy-start.4 = (f32[64,32]{0,1:T(8,128)S(1)}, f32[64,32]{0,1:T(8,128)}, u32[]{:S(2)}) copy-start(f32[64,32]{0,1:T(8,128)} %param.18) | copy-start | bytes 24580
  2.0 12.7 %copy-start.5 = (f32[1024]{0:T(1024)S(1)}, f32[1024]{0:T(1024)}, u32[]{:S(2)}) copy-start(f32[1024]{0:T(1024)} %param.15) | copy-start | bytes 12292
  2.0 12.7 %copy-start.7 = (s32[32]{0:T(128)S(1)}, s32[32]{0:T(128)}, u32[]{:S(2)}) copy-start(s32[32]{0:T(128)} %param.17) | copy-start | bytes 388
  3.2 55.3 %copy-start.3 = (f32[32,1024]{1,0:T(8,128)S(1)}, f32[32,1024]{1,0:T(8,128)}, u32[]{:S(2)}) copy-start(f32[32,1024]{1,0:T(8,128)} %inverse_ref.2) | copy-start | bytes 393220
  3.2 21.3 %all-to-all-start = ((s32[128,1,128]{2,1,0:T(1,128)}), s32[128,1,128]{2,1,0:T(1,128)S(1)}, u32[]{:S(2)}, u32[]{:S(2)}) async-start(s32[128,1,128]{2,1,0:T(1,128)} %bitcast.3), calls=%async_computation | async-start | bytes 131072 | tf_op jit(solution)/shard_map/all_to_all | solution.py:481
  44.8 13.6 %all-to-all-start.2 = ((f32[128,1,128]{2,1,0:T(1,128)}), f32[128,1,128]{2,1,0:T(1,128)S(1)}, u32[]{:S(2)}, u32[]{:S(2)}) async-start(f32[128,1,128]{2,1,0:T(1,128)} %bitcast.11), calls=%async_computation.2 | async-start | bytes 131072 | tf_op jit(solution)/shard_map/all_to_all | solution.py:481
  58.4 39.3 %slice-start = ((s8[8388608]{0:T(1024)(128)(4,1)}), s8[4194304]{0:T(1024)(128)(4,1)S(1)}, s32[]{:S(2)}) async-start(s8[8388608]{0:T(1024)(128)(4,1)} %bitcast.25), calls=%async_computation.7 | async-start | bytes 8388608
  78.8 18.9 %slice-start.1 = ((s8[8388608]{0:T(1024)(128)(4,1)}), s8[4194304]{0:T(1024)(128)(4,1)S(1)}, s32[]{:S(2)}) async-start(s8[8388608]{0:T(1024)(128)(4,1)} %bitcast.25), calls=%async_computation.8 | async-start | bytes 8388608
  78.8 18.9 %copy-start.1 = (bf16[64,64,512]{2,1,0:T(8,128)(2,1)S(1)}, bf16[64,64,512]{2,1,0:T(8,128)(2,1)}, u32[]{:S(2)}) copy-start(bf16[64,64,512]{2,1,0:T(8,128)(2,1)} %inverse_ref.3) | copy-start | bytes 12582916
  78.8 18.9 %copy-start.2 = (f32[64,1024]{1,0:T(8,128)S(1)}, f32[64,1024]{1,0:T(8,128)}, u32[]{:S(2)}) copy-start(f32[64,1024]{1,0:T(8,128)} %diagonal_ref.1) | copy-start | bytes 786436
  78.8 18.9 %copy-start.6 = (s32[2,512]{1,0:T(2,128)S(1)}, s32[2,512]{1,0:T(2,128)}, u32[]{:S(2)}) copy-start(s32[2,512]{1,0:T(2,128)} %index_ref.1) | copy-start | bytes 12292

commit v3 on v2

--- a/solution.py
+++ b/solution.py
@@ -47,12 +47,19 @@
     )(*args)
 
 
-def plan_kernel(row_of_ref, request_ref, ids_ref, *, rows):
-    slots = row_of_ref.shape[1]
+def plan_kernel(owner_hbm, row_hbm, request_ref, ids_ref, owner_ref, row_ref, sems):
+    slots = owner_ref.shape[1]
     devices = request_ref.shape[0]
-    row_of = row_of_ref[...]
-    owner = lax.div(row_of, rows)
-    row = row_of - owner * rows
+    copies = [
+        pltpu.make_async_copy(owner_hbm, owner_ref, sems.at[0]),
+        pltpu.make_async_copy(row_hbm, row_ref, sems.at[1]),
+    ]
+    for copy in copies:
+        copy.start()
+    for copy in copies:
+        copy.wait()
+    owner = owner_ref[...]
+    row = row_ref[...]
     named = one_hot(lax.broadcasted_iota(jnp.int32, (devices, slots), 0) == owner)
     before = lax.broadcasted_iota(jnp.int32, (LANES, LANES), 0) < lax.broadcasted_iota(
         jnp.int32, (LANES, LANES), 1
@@ -152,6 +159,8 @@
     prim_ref,
     vector_ref,
     basis_ref,
+    blocks_hbm,
+    kept_ref,
     weights_ref,
     chosen_ref,
     vectors_ref,
@@ -159,12 +168,17 @@
     named_ref,
     gram_ref,
     last_ref,
+    early_ref,
+    sem,
 ):
+    early = pltpu.make_async_copy(blocks_hbm.at[: early_ref.shape[0]], early_ref, sem)
+    early.start()
     slots = ids_ref.shape[1]
     nprim = vector_ref.shape[0]
     devices = named_ref.shape[0]
     prim = as_column(prim_ref[...])[:nprim].astype(jnp.int32)
     chosen = lax.broadcasted_iota(jnp.int32, (nprim, slots), 1) == prim
+    kept_ref[...] = ids_ref[...]
     weights_ref[...] = weight_ref[...]
     chosen_ref[...] = one_hot(chosen)
     vectors_ref[...] = vector_ref[...]
@@ -184,6 +198,7 @@
     fields = [basis_ref[k] for k in range(kb)]
     last_ref[...] = fields[kb - 1]
     store_sums([(fields[i], fields[j]) for i in range(kb) for j in range(i, kb)], gram_ref)
+    early.wait()
 
 
 def restrict_kernel(
@@ -198,20 +213,29 @@
     contrib_ref[...] = jnp.concatenate([square, jnp.zeros((square.shape[0], LANES - nprim), F32)], axis=1)
 
 
-def neumann_kernel(blocks_hbm, restricted_ref, ids_ref, weight_ref, message_ref, piece_ref, blocks_ref, sems):
+def neumann_kernel(
+    early_ref, blocks_hbm, restricted_ref, ids_ref, weight_ref, message_ref, piece_ref, blocks_ref, sems
+):
     width, slots = piece_ref.shape
+    held = early_ref.shape[0]
     copies = []
-    for n in range(width // 8):
-        rows = pl.ds(n * 8, 8)
-        copies.append(pltpu.make_async_copy(blocks_hbm.at[rows], blocks_ref.at[rows], sems.at[n]))
+    for n, first in enumerate(range(held, width, 8)):
+        copies.append(
+            pltpu.make_async_copy(
+                blocks_hbm.at[first : first + 8], blocks_ref.at[first - held : first - held + 8], sems.at[n]
+            )
+        )
     for copy in copies:
         copy.start()
-    for n, copy in enumerate(copies):
-        copy.wait()
-
-        def chunk(c, _, first=n * 8):
+    for first in range(0, width, 8):
+        ref, start = early_ref, first
+        if first >= held:
+            copies[(first - held) // 8].wait()
+            ref, start = blocks_ref, first - held
+
+        def chunk(c, _, ref=ref, start=start, first=first):
             lanes = pl.ds(pl.multiple_of(c * LANES, LANES), LANES)
-            piece_ref[first : first + 8, lanes] = row_tile([blocks_ref], [restricted_ref[:, lanes]], first, lanes)
+            piece_ref[first : first + 8, lanes] = row_tile([ref], [restricted_ref[:, lanes]], start, lanes)
             return 0
 
         lax.fori_loop(0, slots // LANES, chunk, 0)
@@ -480,15 +504,26 @@
         sent = x.reshape(devices, per, LANES)
         return lax.all_to_all(sent, ("stream", "span"), split_axis=0, concat_axis=0, tiled=True).reshape(x.shape)
 
+    anywhere, here = pl.BlockSpec(memory_space=pl.ANY), pl.BlockSpec(memory_space=pltpu.VMEM)
     requests, ids = call(
-        functools.partial(plan_kernel, rows=rows),
+        plan_kernel,
         (shape((devices, LANES), jnp.int32), shape((2, slots), jnp.int32)),
-        owner * rows + row,
+        owner,
+        row,
+        vmem=54,
         flops=20_000_000_000,
-    )
-    weight, chosen, vectors, coarse, named, gram, last = call(
+        in_specs=[anywhere] * 2,
+        scratch_shapes=[
+            pltpu.VMEM((1, slots), jnp.int32),
+            pltpu.VMEM((1, slots), jnp.int32),
+            pltpu.SemaphoreType.DMA((2,)),
+        ],
+    )
+    held = 8
+    ids, weight, chosen, vectors, coarse, named, gram, last, early = call(
         prepare_kernel,
         (
+            shape((2, slots), jnp.int32),
             shape((1, slots), F32),
             shape((nprim, slots), BF16),
             shape((nprim, width), F32),
@@ -496,16 +531,20 @@
             shape((devices, nprim), BF16),
             shape((32, LANES), F32),
             shape((width, rows), F32),
+            shape((held, width, slots), BF16),
         ),
         ids,
         weight,
         prim,
         prim_vector.T,
         basis,
+        local_inverse,
+        vmem=47,
+        in_specs=[here] * 5 + [anywhere],
+        scratch_shapes=[pltpu.SemaphoreType.DMA],
     )
     arrived = exchange(requests, 1)
     asked, sent = call(fetch_kernel, (shape((2 * PAIRS, devices), jnp.int32), message), arrived, last)
-    anywhere, here = pl.BlockSpec(memory_space=pl.ANY), pl.BlockSpec(memory_space=pltpu.VMEM)
     restricted, contrib = call(
         restrict_kernel, (field, square), exchange(sent, PAIRS), ids, weight, chosen, vectors
     )
@@ -513,16 +552,17 @@
     packed = call(
         neumann_kernel,
         message,
+        early,
         local_inverse,
         restricted,
         ids,
         weight,
         vmem=50,
-        in_specs=[anywhere, here, here, here],
+        in_specs=[here, anywhere, here, here, here],
         scratch_shapes=[
             pltpu.VMEM((width, slots), F32),
-            pltpu.VMEM(local_inverse.shape, BF16),
-            pltpu.SemaphoreType.DMA((width // 8,)),
+            pltpu.VMEM((width - held, width, slots), BF16),
+            pltpu.SemaphoreType.DMA(((width - held) // 8,)),
         ],
     )
     sent = call(

time: 140 us -> 139 us (level)
  no operation moved by 1% of the time
where the time goes in v3:
time: 139 us; the launch traced here: 138 us
  blocking collectives  85.2 us (61%)
  Pallas kernels  23.9 us (17%)
  starting transfers between devices  15.1 us (11%)
  waiting for transfers between devices  12.7 us (9%)
    all_to_all x5, blocking collectives, exchange(): lax.all_to_all(sent, ('stream', 'span'), split_axis=0, concat_axis=0, til...  85.2 us
    pallas_call x10, Pallas kernels, call(): pl.pallas_call(kernel, out_shape=out_shape, compiler_params=pltpu.Compile...  23.9 us
    all_to_all x2, starting transfers between devices, exchange(): lax.all_to_all(sent, ('stream', 'span'), split_axis=0, concat_axis=0, til...  15.1 us
    all_to_all x2, waiting for transfers between devices, exchange(): lax.all_to_all(sent, ('stream', 'span'), split_axis=0, concat_axis=0, til...  12.7 us
  transfers between devices with their start and end apart: 2, of which 2 were waited for; matrix products, arithmetic and copies ran while one was open for 0% of the time, Pallas kernels for 5%

profile of v3, /device:TPU:1, one launch (start us, length us, event | category | flops | bytes accessed | tf_op | source)
XLA Modules:
  0.0 138.5 jit_solution(16659686809179233062)
XLA Ops:
  0.6 0.0 copy-start
  0.6 0.0 copy-start.4
  0.7 0.0 copy-start.6
  0.7 0.0 copy-start.8
  0.7 1.9 %shard_map.131 = (s32[128,128]{1,0:T(8,128)}, s32[2,1024]{1,0:T(2,128)}) custom-call(s32[1,1024]{1,0:T(1,128)} %bitcast.43, s32[1,1024]{1,0:T(1,128)} %bitcast.44), custom_call_target="tpu_custom_call" | custom-call | flops 20000000000 | bytes 200000000 | tf_op jit(solution)/shard_map/pallas_call | solution.py:42
  2.6 11.5 %all-to-all-start = ((s32[128,1,128]{2,1,0:T(1,128)}), s32[128,1,128]{2,1,0:T(1,128)S(1)}, u32[]{:S(2)}, u32[]{:S(2)}) async-start(s32[128,1,128]{2,1,0:T(1,128)} %bitcast.42), calls=%async_computation | async-start | bytes 131072 | tf_op jit(solution)/shard_map/all_to_all | solution.py:505
  14.1 0.0 copy-done
  14.1 0.0 copy-done.4
  14.1 0.0 copy-done.6
  14.2 0.0 copy-done.8
  14.2 0.0 copy-start.5
  14.2 0.7 copy-done.5
  14.9 1.3 shard_map.132
  16.1 7.8 %all-to-all-done = s32[128,1,128]{2,1,0:T(1,128)S(1)} async-done(((s32[128,1,128]{2,1,0:T(1,128)}), s32[128,1,128]{2,1,0:T(1,128)S(1)}, u32[]{:S(2)}, u32[]{:S(2)}) %all-to-all-start) | async-done | bytes 65568 | tf_op jit(solution)/shard_map/all_to_all | solution.py:505
  23.9 0.6 shard_map.133
  24.5 17.9 %all_to_all.35 = f32[128,8,128]{2,1,0:T(8,128)S(1)} all-to-all(f32[128,8,128]{2,1,0:T(8,128)S(1)} %bitcast.32), channel_id=1, replica_groups=mesh['stream'=32,'span'=4] {'stream','span'}, dimensions={0} | all-to-all | bytes 1048576 | tf_op jit(solution)/shard_map/all_to_all | solution.py:505
  42.4 1.8 %shard_map.134 = (f32[64,1024]{1,0:T(8,128)S(1)}, f32[128,128]{1,0:T(8,128)}) custom-call(f32[1024,128]{1,0:T(8,128)S(1)} %bitcast.30, s32[2,1024]{1,0:T(2,128)S(1)} %get-tuple-element.24.ids_ref, f32[1,1024]{1,0:T(1,128)S(1)} %get-tuple-element.25.weight_ref, bf16[32,1024]{1,0:T(8,128)(2,1)S(1)} %get-tuple-element.26.chosen_ref, ...), custom_call_target="tpu_custom_call" | custom-call | tf_op jit(solution)/shard_map/pallas_call | solution.py:42
  44.3 3.6 %all-to-all-start.2 = ((f32[128,1,128]{2,1,0:T(1,128)}), f32[128,1,128]{2,1,0:T(1,128)S(1)}, u32[]{:S(2)}, u32[]{:S(2)}) async-start(f32[128,1,128]{2,1,0:T(1,128)} %bitcast.11), calls=%async_computation.2 | async-start | bytes 131072 | tf_op jit(solution)/shard_map/all_to_all | solution.py:505
  47.9 5.1 %shard_map.135.packed_ref = f32[1024,128]{1,0:T(8,128)S(1)} custom-call(bf16[8,64,1024]{2,1,0:T(8,128)(2,1)S(1)} %get-tuple-element.20.early_ref, bf16[64,64,1024]{2,1,0:T(8,128)(2,1)} %blocks_hbm.3, f32[64,1024]{1,0:T(8,128)S(1)} %get-tuple-element.28.restricted_ref, s32[2,1024]{1,0:T(2,128)S(1)} %get-tuple-element.24.ids_ref, ...), custom_call_target="tpu_custom_call" | custom-call | tf_op jit(solution)/shard_map/pallas_call | solution.py:42
  53.0 4.9 %all-to-all-done.2 = f32[128,1,128]{2,1,0:T(1,128)S(1)} async-done(((f32[128,1,128]{2,1,0:T(1,128)}), f32[128,1,128]{2,1,0:T(1,128)S(1)}, u32[]{:S(2)}, u32[]{:S(2)}) %all-to-all-start.2) | async-done | bytes 65568 | tf_op jit(solution)/shard_map/all_to_all | solution.py:505
  57.9 0.0 copy-done.3
  57.9 0.9 shard_map.136
  58.8 19.0 %all_to_all.36 = f32[128,8,128]{2,1,0:T(8,128)S(1)} all-to-all(f32[128,8,128]{2,1,0:T(8,128)S(1)} %bitcast.31), channel_id=1, replica_groups=mesh['stream'=32,'span'=4] {'stream','span'}, dimensions={0} | all-to-all | bytes 1048576 | tf_op jit(solution)/shard_map/all_to_all | solution.py:505
  77.8 1.3 shard_map.137
  79.2 17.6 %all_to_all.37 = f32[128,8,128]{2,1,0:T(8,128)S(1)} all-to-all(f32[128,8,128]{2,1,0:T(8,128)S(1)} %bitcast.34), channel_id=1, replica_groups=mesh['stream'=32,'span'=4] {'stream','span'}, dimensions={0} | all-to-all | bytes 1048576 | tf_op jit(solution)/shard_map/all_to_all | solution.py:505
  96.7 0.0 slice-done
  96.7 0.0 slice-done.1
  96.8 8.1 %shard_map.138 = f32[1024,128]{1,0:T(8,128)S(1)} custom-call(f32[1024,128]{1,0:T(8,128)S(1)} %bitcast.27, s32[2,1024]{1,0:T(2,128)S(1)} %get-tuple-element.24.ids_ref, s32[2,512]{1,0:T(2,128)S(1)} %copy-done.7, f32[64,1024]{1,0:T(8,128)S(1)} %copy-done.2, bf16[2,64,64,512]{3,2,1,0:T(8,128)(2,1)S(1)} %bitcast.26, bf16[64,64,512]{2,1,0:T(8,128)(2,1)S(1)} %copy-done.1), custom_call_target="tpu_custom_call" | custom-call | tf_op jit(solution)/shard_map/pallas_call | solution.py:42
  104.9 17.5 %all_to_all.38 = f32[128,8,128]{2,1,0:T(8,128)S(1)} all-to-all(f32[128,8,128]{2,1,0:T(8,128)S(1)} %bitcast.28), channel_id=1, replica_groups=mesh['stream'=32,'span'=4] {'stream','span'}, dimensions={0} | all-to-all | bytes 1048576 | tf_op jit(solution)/shard_map/all_to_all | solution.py:505
  122.4 1.5 %shard_map.139 = (f32[64,512]{1,0:T(8,128)S(1)}, f32[128,128]{1,0:T(8,128)S(1)}) custom-call(f32[1024,128]{1,0:T(8,128)S(1)} %bitcast.29, s32[16,128]{1,0:T(8,128)S(1)} %get-tuple-element.32.asked_ref, f32[4,64,512]{2,1,0:T(8,128)S(1)} %copy-done, f32[32,128]{1,0:T(8,128)S(1)} %get-tuple-element.33.gram_ref), custom_call_target="tpu_custom_call" | custom-call | tf_op jit(solution)/shard_map/pallas_call | solution.py:42
  123.9 13.2 %all_to_all.39 = f32[128,1,128]{2,1,0:T(1,128)S(1)} all-to-all(f32[128,1,128]{2,1,0:T(1,128)S(1)} %bitcast.38), channel_id=1, replica_groups=mesh['stream'=32,'span'=4] {'stream','span'}, dimensions={0} | all-to-all | bytes 131072 | tf_op jit(solution)/shard_map/all_to_all | solution.py:505
  137.2 1.3 shard_map.140
  (10 shorter events, 0.0 us)
Async XLA Ops:
  0.6 13.5 %copy-start = (f32[4,64,512]{2,1,0:T(8,128)S(1)}, f32[4,64,512]{2,1,0:T(8,128)}, u32[]{:S(2)}) copy-start(f32[4,64,512]{2,1,0:T(8,128)} %basis_ref.5) | copy-start | bytes 1572868
  0.6 13.5 %copy-start.4 = (f32[64,32]{0,1:T(8,128)S(1)}, f32[64,32]{0,1:T(8,128)}, u32[]{:S(2)}) copy-start(f32[64,32]{0,1:T(8,128)} %param.18) | copy-start | bytes 24580
  0.7 13.5 %copy-start.6 = (f32[1024]{0:T(1024)S(1)}, f32[1024]{0:T(1024)}, u32[]{:S(2)}) copy-start(f32[1024]{0:T(1024)} %param.15) | copy-start | bytes 12292
  0.7 13.5 %copy-start.8 = (s32[32]{0:T(128)S(1)}, s32[32]{0:T(128)}, u32[]{:S(2)}) copy-start(s32[32]{0:T(128)} %param.17) | copy-start | bytes 388
  2.6 21.3 %all-to-all-start = ((s32[128,1,128]{2,1,0:T(1,128)}), s32[128,1,128]{2,1,0:T(1,128)S(1)}, u32[]{:S(2)}, u32[]{:S(2)}) async-start(s32[128,1,128]{2,1,0:T(1,128)} %bitcast.42), calls=%async_computation | async-start | bytes 131072 | tf_op jit(solution)/shard_map/all_to_all | solution.py:505
  14.2 0.7 copy-start.5
  14.9 43.0 %copy-start.3 = (f32[32,1024]{1,0:T(8,128)S(1)}, f32[32,1024]{1,0:T(8,128)}, u32[]{:S(2)}) copy-start(f32[32,1024]{1,0:T(8,128)} %inverse_ref.2) | copy-start | bytes 393220
  44.3 13.6 %all-to-all-start.2 = ((f32[128,1,128]{2,1,0:T(1,128)}), f32[128,1,128]{2,1,0:T(1,128)S(1)}, u32[]{:S(2)}, u32[]{:S(2)}) async-start(f32[128,1,128]{2,1,0:T(1,128)} %bitcast.11), calls=%async_computation.2 | async-start | bytes 131072 | tf_op jit(solution)/shard_map/all_to_all | solution.py:505
  57.9 38.9 %slice-start = ((s8[8388608]{0:T(1024)(128)(4,1)}), s8[4194304]{0:T(1024)(128)(4,1)S(1)}, s32[]{:S(2)}) async-start(s8[8388608]{0:T(1024)(128)(4,1)} %bitcast.25), calls=%async_computation.7 | async-start | bytes 8388608
  77.8 18.9 %slice-start.1 = ((s8[8388608]{0:T(1024)(128)(4,1)}), s8[4194304]{0:T(1024)(128)(4,1)S(1)}, s32[]{:S(2)}) async-start(s8[8388608]{0:T(1024)(128)(4,1)} %bitcast.25), calls=%async_computation.8 | async-start | bytes 8388608
  77.8 18.9 %copy-start.1 = (bf16[64,64,512]{2,1,0:T(8,128)(2,1)S(1)}, bf16[64,64,512]{2,1,0:T(8,128)(2,1)}, u32[]{:S(2)}) copy-start(bf16[64,64,512]{2,1,0:T(8,128)(2,1)} %inverse_ref.3) | copy-start | bytes 12582916
  77.8 18.9 %copy-start.2 = (f32[64,1024]{1,0:T(8,128)S(1)}, f32[64,1024]{1,0:T(8,128)}, u32[]{:S(2)}) copy-start(f32[64,1024]{1,0:T(8,128)} %diagonal_ref.1) | copy-start | bytes 786436
  77.8 18.9 %copy-start.7 = (s32[2,512]{1,0:T(2,128)S(1)}, s32[2,512]{1,0:T(2,128)}, u32[]{:S(2)}) copy-start(s32[2,512]{1,0:T(2,128)} %index_ref.1) | copy-start | bytes 12292

commit v4 on v3

--- a/solution.py
+++ b/solution.py
@@ -130,10 +130,14 @@
 
 
 def row_tile(block_refs, vectors, first, lanes):
+    return tile_of([(block_refs, first + j) for j in range(8)], vectors, lanes)
+
+
+def tile_of(places, vectors, lanes):
     row = lax.broadcasted_iota(jnp.int32, (8, LANES), 0)
     result = jnp.zeros((8, LANES), F32)
-    for j in range(8):
-        result = jnp.where(row == j, block_sums(block_refs, vectors, first + j, lanes), result)
+    for j, (refs, a) in enumerate(places):
+        result = jnp.where(row == j, block_sums(refs, vectors, a, lanes), result)
     return result
 
 
@@ -197,7 +201,9 @@
     kb = basis_ref.shape[0]
     fields = [basis_ref[k] for k in range(kb)]
     last_ref[...] = fields[kb - 1]
-    store_sums([(fields[i], fields[j]) for i in range(kb) for j in range(i, kb)], gram_ref)
+    total, rest = lane_sums([(fields[i], fields[j]) for i in range(kb) for j in range(i, kb)])
+    lane = lax.broadcasted_iota(jnp.int32, (8, LANES), 1)
+    gram_ref[...] = jnp.where(lane < 32, pltpu.roll(total, 16, 1), pltpu.roll(rest, 32, 1))
     early.wait()
 
 
@@ -218,24 +224,23 @@
 ):
     width, slots = piece_ref.shape
     held = early_ref.shape[0]
-    copies = []
-    for n, first in enumerate(range(held, width, 8)):
-        copies.append(
-            pltpu.make_async_copy(
-                blocks_hbm.at[first : first + 8], blocks_ref.at[first - held : first - held + 8], sems.at[n]
-            )
+    copies = {}
+    for first in range(held // 8 * 8, width, 8):
+        start = max(first - held, 0)
+        rows = pl.ds(start, first + 8 - held - start)
+        copies[first] = pltpu.make_async_copy(
+            blocks_hbm.at[pl.ds(start + held, first + 8 - held - start)], blocks_ref.at[rows], sems.at[first // 8]
         )
-    for copy in copies:
+    for copy in copies.values():
         copy.start()
     for first in range(0, width, 8):
-        ref, start = early_ref, first
-        if first >= held:
-            copies[(first - held) // 8].wait()
-            ref, start = blocks_ref, first - held
-
-        def chunk(c, _, ref=ref, start=start, first=first):
+        if first in copies:
+            copies[first].wait()
+        places = [([early_ref], a) if a < held else ([blocks_ref], a - held) for a in range(first, first + 8)]
+
+        def chunk(c, _, places=places, first=first):
             lanes = pl.ds(pl.multiple_of(c * LANES, LANES), LANES)
-            piece_ref[first : first + 8, lanes] = row_tile([ref], [restricted_ref[:, lanes]], start, lanes)
+            piece_ref[first : first + 8, lanes] = tile_of(places, [restricted_ref[:, lanes]], lanes)
             return 0
 
         lax.fori_loop(0, slots // LANES, chunk, 0)
@@ -383,7 +388,7 @@
     return product, ((a_high * b_high - product) + a_high * b_low + a_low * b_high) + a_low * b_low
 
 
-def store_sums(products, out_ref):
+def lane_sums(products):
     row = lax.broadcasted_iota(jnp.int32, (8, LANES), 0)
     tiles = []
     for base in range(0, len(products), 8):
@@ -399,28 +404,27 @@
             for shift in (4, 2, 1):
                 pair = pair_add(pair, tuple(pltpu.roll(p, shift, 0) for p in pair))
             tile = tuple(jnp.where(row == n, p, t) for p, t in zip(pair, tile))
-        shift = LANES // 2
-        while shift:
-            tile = pair_add(tile, tuple(pltpu.roll(t, shift, 1) for t in tile))
-            shift //= 2
         tiles.append(tile)
-    half = out_ref.shape[0] // 2
-    for n, tile in enumerate(tiles):
-        out_ref[n * 8 : (n + 1) * 8, :] = tile[0]
-        out_ref[half + n * 8 : half + (n + 1) * 8, :] = tile[1]
-    for n in range(len(tiles), half // 8):
-        out_ref[n * 8 : (n + 1) * 8, :] = jnp.zeros((8, LANES), F32)
-        out_ref[half + n * 8 : half + (n + 1) * 8, :] = jnp.zeros((8, LANES), F32)
-
-
-def final_kernel(arrived_ref, asked_ref, basis_ref, gram_ref, image_ref, stats_ref, sums_ref):
+    pad = [jnp.zeros((LANES - 8 * len(tiles), LANES), F32)]
+    pair = tuple(jnp.concatenate([tile[part] for tile in tiles] + pad, axis=0).T for part in range(2))
+    half = LANES // 2
+    while half >= 8:
+        pair = pair_add(tuple(p[:half] for p in pair), tuple(p[half:] for p in pair))
+        half //= 2
+    for shift in (4, 2, 1):
+        pair = pair_add(pair, tuple(pltpu.roll(p, shift, 0) for p in pair))
+    return pair
+
+
+def final_kernel(arrived_ref, asked_ref, basis_ref, gram_ref, image_ref, stats_ref):
     kb, width, rows = basis_ref.shape
     image = rows_from_messages(arrived_ref, asked_ref[...], rows)
     image_ref[...] = image
-    store_sums([(image, image)] + [(image, basis_ref[k]) for k in range(kb)], sums_ref)
-    used = sums_ref.shape[0] + gram_ref.shape[0]
-    square = jnp.concatenate([sums_ref[...], gram_ref[...], jnp.zeros((LANES - used, LANES), F32)], axis=0)
-    stats_ref[...] = square.T
+    total, rest = lane_sums([(image, image)] + [(image, basis_ref[k]) for k in range(kb)])
+    lane = lax.broadcasted_iota(jnp.int32, (8, LANES), 1)
+    row = jnp.where(lane < 8, total, pltpu.roll(rest, 8, 1))
+    row = jnp.where(lane < 16, row, gram_ref[...])
+    stats_ref[...] = jnp.concatenate([row] * (stats_ref.shape[0] // 8), axis=0)
 
 
 def finish_kernel(gathered_ref, image_ref, basis_ref, direction_ref, coeff_ref, *, entries):
@@ -465,7 +469,7 @@
     remainder = image_ref[...]
     for k in range(kb):
         remainder = remainder - steps[k] * basis_ref[k]
-    direction_ref[...] = remainder / root_mean
+    direction_ref[...] = remainder * (1.0 / root_mean)
     values = jnp.where(lane == kb, root_mean, pltpu.roll(projected, LANES - 1, 1))
     coeff_ref[...] = values[0, : kb + 1]
 
@@ -519,7 +523,7 @@
             pltpu.SemaphoreType.DMA((2,)),
         ],
     )
-    held = 8
+    held = 14
     ids, weight, chosen, vectors, coarse, named, gram, last, early = call(
         prepare_kernel,
         (
@@ -529,7 +533,7 @@
             shape((nprim, width), F32),
             shape((PAIRS * nprim, LANES), F32),
             shape((devices, nprim), BF16),
-            shape((32, LANES), F32),
+            shape((8, LANES), F32),
             shape((width, rows), F32),
             shape((held, width, slots), BF16),
         ),
@@ -562,7 +566,7 @@
         scratch_shapes=[
             pltpu.VMEM((width, slots), F32),
             pltpu.VMEM((width - held, width, slots), BF16),
-            pltpu.SemaphoreType.DMA(((width - held) // 8,)),
+            pltpu.SemaphoreType.DMA((width // 8,)),
         ],
     )
     sent = call(
@@ -597,7 +601,6 @@
         asked,
         basis,
         gram,
-        scratch_shapes=[pltpu.VMEM((16, LANES), F32)],
     )
     return call(
         functools.partial(finish_kernel, entries=entries),

time: 139 us -> 138 us (level)
  no operation moved by 1% of the time
where the time goes in v4:
time: 138 us
  blocking collectives  84.9 us (62%)
  Pallas kernels  23.9 us (17%)
  starting transfers between devices  15.1 us (11%)
  waiting for transfers between devices  12.3 us (9%)
    all_to_all x5, blocking collectives, exchange(): lax.all_to_all(sent, ('stream', 'span'), split_axis=0, concat_axis=0, til...  84.9 us
    pallas_call x10, Pallas kernels, call(): pl.pallas_call(kernel, out_shape=out_shape, compiler_params=pltpu.Compile...  23.9 us
    all_to_all x2, starting transfers between devices, exchange(): lax.all_to_all(sent, ('stream', 'span'), split_axis=0, concat_axis=0, til...  15.1 us
    all_to_all x2, waiting for transfers between devices, exchange(): lax.all_to_all(sent, ('stream', 'span'), split_axis=0, concat_axis=0, til...  12.3 us
  transfers between devices with their start and end apart: 2, of which 2 were waited for; matrix products, arithmetic and copies ran while one was open for 0% of the time, Pallas kernels for 5%

profile of v4, /device:TPU:1, one launch (start us, length us, event | category | flops | bytes accessed | tf_op | source)
XLA Modules:
  0.0 137.8 jit_solution(11684316622017807652)
XLA Ops:
  0.6 0.0 copy-start
  0.6 0.0 copy-start.4
  0.7 0.0 copy-start.6
  0.7 0.0 copy-start.8
  0.7 1.9 %shard_map.131 = (s32[128,128]{1,0:T(8,128)}, s32[2,1024]{1,0:T(2,128)}) custom-call(s32[1,1024]{1,0:T(1,128)} %bitcast.43, s32[1,1024]{1,0:T(1,128)} %bitcast.44), custom_call_target="tpu_custom_call" | custom-call | flops 20000000000 | bytes 200000000 | tf_op jit(solution)/shard_map/pallas_call | solution.py:42
  2.6 11.5 %all-to-all-start = ((s32[128,1,128]{2,1,0:T(1,128)}), s32[128,1,128]{2,1,0:T(1,128)S(1)}, u32[]{:S(2)}, u32[]{:S(2)}) async-start(s32[128,1,128]{2,1,0:T(1,128)} %bitcast.42), calls=%async_computation | async-start | bytes 131072 | tf_op jit(solution)/shard_map/all_to_all | solution.py:509
  14.1 0.0 copy-done
  14.1 0.0 copy-done.4
  14.1 0.0 copy-done.6
  14.2 0.0 copy-done.8
  14.2 0.0 copy-start.5
  14.2 0.7 copy-done.5
  14.9 1.9 %shard_map.132 = (s32[2,1024]{1,0:T(2,128)S(1)}, f32[1,1024]{1,0:T(1,128)S(1)}, bf16[32,1024]{1,0:T(8,128)(2,1)S(1)}, f32[32,64]{1,0:T(8,128)S(1)}, f32[256,128]...) custom-call(s32[2,1024]{1,0:T(2,128)S(1)} %copy-done.5, ...), custom_call_target="tpu_custom_call" | custom-call | tf_op jit(solution)/shard_map/pallas_call | solution.py:42
  16.8 0.0 copy-start.3
  16.8 7.2 %all-to-all-done = s32[128,1,128]{2,1,0:T(1,128)S(1)} async-done(((s32[128,1,128]{2,1,0:T(1,128)}), s32[128,1,128]{2,1,0:T(1,128)S(1)}, u32[]{:S(2)}, u32[]{:S(2)}) %all-to-all-start) | async-done | bytes 65568 | tf_op jit(solution)/shard_map/all_to_all | solution.py:509
  23.9 0.6 shard_map.133
  24.5 17.9 %all_to_all.35 = f32[128,8,128]{2,1,0:T(8,128)S(1)} all-to-all(f32[128,8,128]{2,1,0:T(8,128)S(1)} %bitcast.32), channel_id=1, replica_groups=mesh['stream'=32,'span'=4] {'stream','span'}, dimensions={0} | all-to-all | bytes 1048576 | tf_op jit(solution)/shard_map/all_to_all | solution.py:509
  42.4 1.8 %shard_map.134 = (f32[64,1024]{1,0:T(8,128)S(1)}, f32[128,128]{1,0:T(8,128)}) custom-call(f32[1024,128]{1,0:T(8,128)S(1)} %bitcast.30, s32[2,1024]{1,0:T(2,128)S(1)} %get-tuple-element.24.ids_ref, f32[1,1024]{1,0:T(1,128)S(1)} %get-tuple-element.25.weight_ref, bf16[32,1024]{1,0:T(8,128)(2,1)S(1)} %get-tuple-element.26.chosen_ref, ...), custom_call_target="tpu_custom_call" | custom-call | tf_op jit(solution)/shard_map/pallas_call | solution.py:42
  44.3 3.6 %all-to-all-start.2 = ((f32[128,1,128]{2,1,0:T(1,128)}), f32[128,1,128]{2,1,0:T(1,128)S(1)}, u32[]{:S(2)}, u32[]{:S(2)}) async-start(f32[128,1,128]{2,1,0:T(1,128)} %bitcast.11), calls=%async_computation.2 | async-start | bytes 131072 | tf_op jit(solution)/shard_map/all_to_all | solution.py:509
  47.9 4.8 %shard_map.135.packed_ref = f32[1024,128]{1,0:T(8,128)S(1)} custom-call(bf16[14,64,1024]{2,1,0:T(8,128)(2,1)S(1)} %get-tuple-element.20.early_ref, bf16[64,64,1024]{2,1,0:T(8,128)(2,1)} %blocks_hbm.3, f32[64,1024]{1,0:T(8,128)S(1)} %get-tuple-element.28.restricted_ref, s32[2,1024]{1,0:T(2,128)S(1)} %get-tuple-element.24.ids_ref, ...), custom_call_target="tpu_custom_call" | custom-call | tf_op jit(solution)/shard_map/pallas_call | solution.py:42
  52.7 5.2 %all-to-all-done.2 = f32[128,1,128]{2,1,0:T(1,128)S(1)} async-done(((f32[128,1,128]{2,1,0:T(1,128)}), f32[128,1,128]{2,1,0:T(1,128)S(1)}, u32[]{:S(2)}, u32[]{:S(2)}) %all-to-all-start.2) | async-done | bytes 65568 | tf_op jit(solution)/shard_map/all_to_all | solution.py:509
  57.9 0.9 shard_map.136
  58.8 18.7 %all_to_all.36 = f32[128,8,128]{2,1,0:T(8,128)S(1)} all-to-all(f32[128,8,128]{2,1,0:T(8,128)S(1)} %bitcast.31), channel_id=1, replica_groups=mesh['stream'=32,'span'=4] {'stream','span'}, dimensions={0} | all-to-all | bytes 1048576 | tf_op jit(solution)/shard_map/all_to_all | solution.py:509
  77.6 1.3 shard_map.137
  78.9 17.6 %all_to_all.37 = f32[128,8,128]{2,1,0:T(8,128)S(1)} all-to-all(f32[128,8,128]{2,1,0:T(8,128)S(1)} %bitcast.34), channel_id=1, replica_groups=mesh['stream'=32,'span'=4] {'stream','span'}, dimensions={0} | all-to-all | bytes 1048576 | tf_op jit(solution)/shard_map/all_to_all | solution.py:509
  96.5 0.0 copy-done.2
  96.5 0.0 copy-done.7
  96.5 8.1 %shard_map.138 = f32[1024,128]{1,0:T(8,128)S(1)} custom-call(f32[1024,128]{1,0:T(8,128)S(1)} %bitcast.27, s32[2,1024]{1,0:T(2,128)S(1)} %get-tuple-element.24.ids_ref, s32[2,512]{1,0:T(2,128)S(1)} %copy-done.7, f32[64,1024]{1,0:T(8,128)S(1)} %copy-done.2, bf16[2,64,64,512]{3,2,1,0:T(8,128)(2,1)S(1)} %bitcast.26, bf16[64,64,512]{2,1,0:T(8,128)(2,1)S(1)} %copy-done.1), custom_call_target="tpu_custom_call" | custom-call | tf_op jit(solution)/shard_map/pallas_call | solution.py:42
  104.7 17.5 %all_to_all.38 = f32[128,8,128]{2,1,0:T(8,128)S(1)} all-to-all(f32[128,8,128]{2,1,0:T(8,128)S(1)} %bitcast.28), channel_id=1, replica_groups=mesh['stream'=32,'span'=4] {'stream','span'}, dimensions={0} | all-to-all | bytes 1048576 | tf_op jit(solution)/shard_map/all_to_all | solution.py:509
  122.2 1.1 shard_map.139
  123.3 13.2 %all_to_all.39 = f32[128,1,128]{2,1,0:T(1,128)S(1)} all-to-all(f32[128,1,128]{2,1,0:T(1,128)S(1)} %bitcast.38), channel_id=1, replica_groups=mesh['stream'=32,'span'=4] {'stream','span'}, dimensions={0} | all-to-all | bytes 131072 | tf_op jit(solution)/shard_map/all_to_all | solution.py:509
  136.5 1.3 shard_map.140
  (10 shorter events, 0.0 us)
Async XLA Ops:
  0.6 13.5 %copy-start = (f32[4,64,512]{2,1,0:T(8,128)S(1)}, f32[4,64,512]{2,1,0:T(8,128)}, u32[]{:S(2)}) copy-start(f32[4,64,512]{2,1,0:T(8,128)} %basis_ref.5) | copy-start | bytes 1572868
  0.6 13.5 %copy-start.4 = (f32[64,32]{0,1:T(8,128)S(1)}, f32[64,32]{0,1:T(8,128)}, u32[]{:S(2)}) copy-start(f32[64,32]{0,1:T(8,128)} %param.18) | copy-start | bytes 24580
  0.7 13.5 %copy-start.6 = (f32[1024]{0:T(1024)S(1)}, f32[1024]{0:T(1024)}, u32[]{:S(2)}) copy-start(f32[1024]{0:T(1024)} %param.15) | copy-start | bytes 12292
  0.7 13.5 %copy-start.8 = (s32[32]{0:T(128)S(1)}, s32[32]{0:T(128)}, u32[]{:S(2)}) copy-start(s32[32]{0:T(128)} %param.17) | copy-start | bytes 388
  2.6 21.3 %all-to-all-start = ((s32[128,1,128]{2,1,0:T(1,128)}), s32[128,1,128]{2,1,0:T(1,128)S(1)}, u32[]{:S(2)}, u32[]{:S(2)}) async-start(s32[128,1,128]{2,1,0:T(1,128)} %bitcast.42), calls=%async_computation | async-start | bytes 131072 | tf_op jit(solution)/shard_map/all_to_all | solution.py:509
  14.2 0.7 copy-start.5
  16.8 41.1 %copy-start.3 = (f32[32,1024]{1,0:T(8,128)S(1)}, f32[32,1024]{1,0:T(8,128)}, u32[]{:S(2)}) copy-start(f32[32,1024]{1,0:T(8,128)} %inverse_ref.2) | copy-start | bytes 393220
  44.3 13.6 %all-to-all-start.2 = ((f32[128,1,128]{2,1,0:T(1,128)}), f32[128,1,128]{2,1,0:T(1,128)S(1)}, u32[]{:S(2)}, u32[]{:S(2)}) async-start(f32[128,1,128]{2,1,0:T(1,128)} %bitcast.11), calls=%async_computation.2 | async-start | bytes 131072 | tf_op jit(solution)/shard_map/all_to_all | solution.py:509
  57.9 38.6 %slice-start = ((s8[8388608]{0:T(1024)(128)(4,1)}), s8[4194304]{0:T(1024)(128)(4,1)S(1)}, s32[]{:S(2)}) async-start(s8[8388608]{0:T(1024)(128)(4,1)} %bitcast.25), calls=%async_computation.7 | async-start | bytes 8388608
  77.5 18.9 %slice-start.1 = ((s8[8388608]{0:T(1024)(128)(4,1)}), s8[4194304]{0:T(1024)(128)(4,1)S(1)}, s32[]{:S(2)}) async-start(s8[8388608]{0:T(1024)(128)(4,1)} %bitcast.25), calls=%async_computation.8 | async-start | bytes 8388608
  77.6 18.9 %copy-start.1 = (bf16[64,64,512]{2,1,0:T(8,128)(2,1)S(1)}, bf16[64,64,512]{2,1,0:T(8,128)(2,1)}, u32[]{:S(2)}) copy-start(bf16[64,64,512]{2,1,0:T(8,128)(2,1)} %inverse_ref.3) | copy-start | bytes 12582916
  77.6 18.9 %copy-start.2 = (f32[64,1024]{1,0:T(8,128)S(1)}, f32[64,1024]{1,0:T(8,128)}, u32[]{:S(2)}) copy-start(f32[64,1024]{1,0:T(8,128)} %diagonal_ref.1) | copy-start | bytes 786436
  77.6 18.9 %copy-start.7 = (s32[2,512]{1,0:T(2,128)S(1)}, s32[2,512]{1,0:T(2,128)}, u32[]{:S(2)}) copy-start(s32[2,512]{1,0:T(2,128)} %index_ref.1) | copy-start | bytes 12292

commit v5 on v4

--- a/solution.py
+++ b/solution.py
@@ -95,13 +95,13 @@
         lanes = slice(c * chunk, (c + 1) * chunk)
         named = one_hot(lax.broadcasted_iota(jnp.int32, (devices, chunk), 0) == owner[:, lanes])
         named = jnp.concatenate([named, named], axis=0)
-        place = jnp.broadcast_to(rank[:, lanes], (width, chunk))
-        total = jnp.zeros((width, chunk), F32)
+        place = jnp.broadcast_to(rank[:, lanes], (8, chunk))
+        total = jnp.zeros((width // 8, 8, chunk), F32)
         for k in range(PAIRS):
-            both = mm(sides[k], named)
-            total = jnp.where(place == 2 * k, both[:width], total)
-            total = jnp.where(place == 2 * k + 1, both[width:], total)
-        pieces.append(total)
+            both = mm(sides[k], named).reshape(width // 4, 8, chunk)
+            total = jnp.where((place == 2 * k)[None], both[: width // 8], total)
+            total = jnp.where((place == 2 * k + 1)[None], both[width // 8 :], total)
+        pieces.append(total.reshape(width, chunk))
     return jnp.concatenate(pieces, axis=1)
 
 
@@ -250,13 +250,15 @@
 def correct_kernel(packed_ref, gathered_ref, inverse_ref, coarse_ref, named_ref, message_ref, *, span):
     devices, nprim = named_ref.shape
     ncs = inverse_ref.shape[1]
-    contrib = gathered_ref[...][:, :nprim]
+    streams = devices // span
+    group = lax.broadcasted_iota(jnp.int32, (streams, devices), 1)
+    group = jnp.where(lax.div(group, span) == lax.broadcasted_iota(jnp.int32, (streams, devices), 0), 1.0, 0.0)
+    contrib = jnp.dot(group, gathered_ref[...], precision=HIGH, preferred_element_type=F32)[:, :nprim]
     lane = lax.broadcasted_iota(jnp.int32, (nprim, ncs), 1)
     spread = jnp.where(lax.rem(lane, nprim) == lax.broadcasted_iota(jnp.int32, (nprim, ncs), 0), 1.0, 0.0)
     tiled = jnp.dot(contrib, spread, precision=HIGH, preferred_element_type=F32)
-    device = lax.broadcasted_iota(jnp.int32, (devices, ncs), 0)
-    stream = lax.broadcasted_iota(jnp.int32, (devices, ncs), 1)
-    mine = lax.div(device, span) == lax.div(stream, nprim)
+    stream = lax.broadcasted_iota(jnp.int32, (streams, ncs), 0)
+    mine = lax.div(lax.broadcasted_iota(jnp.int32, (streams, ncs), 1), nprim) == stream
     coarse_rhs = jnp.sum(jnp.where(mine, tiled, 0.0), axis=0, keepdims=True)
     coarse_sol = jnp.sum(inverse_ref[...] * coarse_rhs, axis=1, keepdims=True)
     for k in range(PAIRS):

time: 138 us -> 138 us (level)
  no operation moved by 1% of the time
where the time goes in v5:
time: 138 us
  blocking collectives  84.9 us (62%)
  Pallas kernels  23.9 us (17%)
  starting transfers between devices  15.1 us (11%)
  waiting for transfers between devices  12.3 us (9%)
    all_to_all x5, blocking collectives, exchange(): lax.all_to_all(sent, ('stream', 'span'), split_axis=0, concat_axis=0, til...  84.9 us
    pallas_call x10, Pallas kernels, call(): pl.pallas_call(kernel, out_shape=out_shape, compiler_params=pltpu.Compile...  23.9 us
    all_to_all x2, starting transfers between devices, exchange(): lax.all_to_all(sent, ('stream', 'span'), split_axis=0, concat_axis=0, til...  15.1 us
    all_to_all x2, waiting for transfers between devices, exchange(): lax.all_to_all(sent, ('stream', 'span'), split_axis=0, concat_axis=0, til...  12.3 us
  transfers between devices with their start and end apart: 2, of which 2 were waited for; matrix products, arithmetic and copies ran while one was open for 0% of the time, Pallas kernels for 5%

profile of v5, /device:TPU:1, one launch (start us, length us, event | category | flops | bytes accessed | tf_op | source)
XLA Modules:
  0.0 137.8 jit_solution(16735834761165144311)
XLA Ops:
  0.6 0.0 copy-start
  0.6 0.0 copy-start.4
  0.7 0.0 copy-start.6
  0.7 0.0 copy-start.8
  0.7 1.9 %shard_map.131 = (s32[128,128]{1,0:T(8,128)}, s32[2,1024]{1,0:T(2,128)}) custom-call(s32[1,1024]{1,0:T(1,128)} %bitcast.43, s32[1,1024]{1,0:T(1,128)} %bitcast.44), custom_call_target="tpu_custom_call" | custom-call | flops 20000000000 | bytes 200000000 | tf_op jit(solution)/shard_map/pallas_call | solution.py:42
  2.6 11.5 %all-to-all-start = ((s32[128,1,128]{2,1,0:T(1,128)}), s32[128,1,128]{2,1,0:T(1,128)S(1)}, u32[]{:S(2)}, u32[]{:S(2)}) async-start(s32[128,1,128]{2,1,0:T(1,128)} %bitcast.42), calls=%async_computation | async-start | bytes 131072 | tf_op jit(solution)/shard_map/all_to_all | solution.py:511
  14.1 0.0 copy-done
  14.1 0.0 copy-done.4
  14.1 0.0 copy-done.6
  14.2 0.0 copy-done.8
  14.2 0.0 copy-start.5
  14.2 0.7 copy-done.5
  14.9 1.9 %shard_map.132 = (s32[2,1024]{1,0:T(2,128)S(1)}, f32[1,1024]{1,0:T(1,128)S(1)}, bf16[32,1024]{1,0:T(8,128)(2,1)S(1)}, f32[32,64]{1,0:T(8,128)S(1)}, f32[256,128]...) custom-call(s32[2,1024]{1,0:T(2,128)S(1)} %copy-done.5, ...), custom_call_target="tpu_custom_call" | custom-call | tf_op jit(solution)/shard_map/pallas_call | solution.py:42
  16.8 0.0 copy-start.3
  16.8 7.2 %all-to-all-done = s32[128,1,128]{2,1,0:T(1,128)S(1)} async-done(((s32[128,1,128]{2,1,0:T(1,128)}), s32[128,1,128]{2,1,0:T(1,128)S(1)}, u32[]{:S(2)}, u32[]{:S(2)}) %all-to-all-start) | async-done | bytes 65568 | tf_op jit(solution)/shard_map/all_to_all | solution.py:511
  23.9 0.6 shard_map.133
  24.5 17.9 %all_to_all.35 = f32[128,8,128]{2,1,0:T(8,128)S(1)} all-to-all(f32[128,8,128]{2,1,0:T(8,128)S(1)} %bitcast.32), channel_id=1, replica_groups=mesh['stream'=32,'span'=4] {'stream','span'}, dimensions={0} | all-to-all | bytes 1048576 | tf_op jit(solution)/shard_map/all_to_all | solution.py:511
  42.4 1.8 %shard_map.134 = (f32[64,1024]{1,0:T(8,128)S(1)}, f32[128,128]{1,0:T(8,128)}) custom-call(f32[1024,128]{1,0:T(8,128)S(1)} %bitcast.30, s32[2,1024]{1,0:T(2,128)S(1)} %get-tuple-element.24.ids_ref, f32[1,1024]{1,0:T(1,128)S(1)} %get-tuple-element.25.weight_ref, bf16[32,1024]{1,0:T(8,128)(2,1)S(1)} %get-tuple-element.26.chosen_ref, ...), custom_call_target="tpu_custom_call" | custom-call | tf_op jit(solution)/shard_map/pallas_call | solution.py:42
  44.3 3.6 %all-to-all-start.2 = ((f32[128,1,128]{2,1,0:T(1,128)}), f32[128,1,128]{2,1,0:T(1,128)S(1)}, u32[]{:S(2)}, u32[]{:S(2)}) async-start(f32[128,1,128]{2,1,0:T(1,128)} %bitcast.11), calls=%async_computation.2 | async-start | bytes 131072 | tf_op jit(solution)/shard_map/all_to_all | solution.py:511
  47.9 4.8 %shard_map.135.packed_ref = f32[1024,128]{1,0:T(8,128)S(1)} custom-call(bf16[14,64,1024]{2,1,0:T(8,128)(2,1)S(1)} %get-tuple-element.20.early_ref, bf16[64,64,1024]{2,1,0:T(8,128)(2,1)} %blocks_hbm.3, f32[64,1024]{1,0:T(8,128)S(1)} %get-tuple-element.28.restricted_ref, s32[2,1024]{1,0:T(2,128)S(1)} %get-tuple-element.24.ids_ref, ...), custom_call_target="tpu_custom_call" | custom-call | tf_op jit(solution)/shard_map/pallas_call | solution.py:42
  52.7 5.2 %all-to-all-done.2 = f32[128,1,128]{2,1,0:T(1,128)S(1)} async-done(((f32[128,1,128]{2,1,0:T(1,128)}), f32[128,1,128]{2,1,0:T(1,128)S(1)}, u32[]{:S(2)}, u32[]{:S(2)}) %all-to-all-start.2) | async-done | bytes 65568 | tf_op jit(solution)/shard_map/all_to_all | solution.py:511
  57.9 0.0 copy-done.3
  57.9 0.9 shard_map.136
  58.8 18.7 %all_to_all.36 = f32[128,8,128]{2,1,0:T(8,128)S(1)} all-to-all(f32[128,8,128]{2,1,0:T(8,128)S(1)} %bitcast.31), channel_id=1, replica_groups=mesh['stream'=32,'span'=4] {'stream','span'}, dimensions={0} | all-to-all | bytes 1048576 | tf_op jit(solution)/shard_map/all_to_all | solution.py:511
  77.5 1.3 shard_map.137
  78.9 17.6 %all_to_all.37 = f32[128,8,128]{2,1,0:T(8,128)S(1)} all-to-all(f32[128,8,128]{2,1,0:T(8,128)S(1)} %bitcast.34), channel_id=1, replica_groups=mesh['stream'=32,'span'=4] {'stream','span'}, dimensions={0} | all-to-all | bytes 1048576 | tf_op jit(solution)/shard_map/all_to_all | solution.py:511
  96.4 0.0 slice-done
  96.5 8.1 %shard_map.138 = f32[1024,128]{1,0:T(8,128)S(1)} custom-call(f32[1024,128]{1,0:T(8,128)S(1)} %bitcast.27, s32[2,1024]{1,0:T(2,128)S(1)} %get-tuple-element.24.ids_ref, s32[2,512]{1,0:T(2,128)S(1)} %copy-done.7, f32[64,1024]{1,0:T(8,128)S(1)} %copy-done.2, bf16[2,64,64,512]{3,2,1,0:T(8,128)(2,1)S(1)} %bitcast.26, bf16[64,64,512]{2,1,0:T(8,128)(2,1)S(1)} %copy-done.1), custom_call_target="tpu_custom_call" | custom-call | tf_op jit(solution)/shard_map/pallas_call | solution.py:42
  104.6 17.5 %all_to_all.38 = f32[128,8,128]{2,1,0:T(8,128)S(1)} all-to-all(f32[128,8,128]{2,1,0:T(8,128)S(1)} %bitcast.28), channel_id=1, replica_groups=mesh['stream'=32,'span'=4] {'stream','span'}, dimensions={0} | all-to-all | bytes 1048576 | tf_op jit(solution)/shard_map/all_to_all | solution.py:511
  122.1 1.1 shard_map.139
  123.2 13.2 %all_to_all.39 = f32[128,1,128]{2,1,0:T(1,128)S(1)} all-to-all(f32[128,1,128]{2,1,0:T(1,128)S(1)} %bitcast.38), channel_id=1, replica_groups=mesh['stream'=32,'span'=4] {'stream','span'}, dimensions={0} | all-to-all | bytes 131072 | tf_op jit(solution)/shard_map/all_to_all | solution.py:511
  136.5 1.3 shard_map.140
  (10 shorter events, 0.0 us)
Async XLA Ops:
  0.6 13.5 %copy-start = (f32[4,64,512]{2,1,0:T(8,128)S(1)}, f32[4,64,512]{2,1,0:T(8,128)}, u32[]{:S(2)}) copy-start(f32[4,64,512]{2,1,0:T(8,128)} %basis_ref.5) | copy-start | bytes 1572868
  0.6 13.5 %copy-start.4 = (f32[64,32]{0,1:T(8,128)S(1)}, f32[64,32]{0,1:T(8,128)}, u32[]{:S(2)}) copy-start(f32[64,32]{0,1:T(8,128)} %param.18) | copy-start | bytes 24580
  0.7 13.5 %copy-start.6 = (f32[1024]{0:T(1024)S(1)}, f32[1024]{0:T(1024)}, u32[]{:S(2)}) copy-start(f32[1024]{0:T(1024)} %param.15) | copy-start | bytes 12292
  0.7 13.5 %copy-start.8 = (s32[32]{0:T(128)S(1)}, s32[32]{0:T(128)}, u32[]{:S(2)}) copy-start(s32[32]{0:T(128)} %param.17) | copy-start | bytes 388
  2.6 21.3 %all-to-all-start = ((s32[128,1,128]{2,1,0:T(1,128)}), s32[128,1,128]{2,1,0:T(1,128)S(1)}, u32[]{:S(2)}, u32[]{:S(2)}) async-start(s32[128,1,128]{2,1,0:T(1,128)} %bitcast.42), calls=%async_computation | async-start | bytes 131072 | tf_op jit(solution)/shard_map/all_to_all | solution.py:511
  14.2 0.7 copy-start.5
  16.8 41.1 %copy-start.3 = (f32[32,1024]{1,0:T(8,128)S(1)}, f32[32,1024]{1,0:T(8,128)}, u32[]{:S(2)}) copy-start(f32[32,1024]{1,0:T(8,128)} %inverse_ref.2) | copy-start | bytes 393220
  44.3 13.6 %all-to-all-start.2 = ((f32[128,1,128]{2,1,0:T(1,128)}), f32[128,1,128]{2,1,0:T(1,128)S(1)}, u32[]{:S(2)}, u32[]{:S(2)}) async-start(f32[128,1,128]{2,1,0:T(1,128)} %bitcast.11), calls=%async_computation.2 | async-start | bytes 131072 | tf_op jit(solution)/shard_map/all_to_all | solution.py:511
  57.9 38.6 %slice-start = ((s8[8388608]{0:T(1024)(128)(4,1)}), s8[4194304]{0:T(1024)(128)(4,1)S(1)}, s32[]{:S(2)}) async-start(s8[8388608]{0:T(1024)(128)(4,1)} %bitcast.25), calls=%async_computation.7 | async-start | bytes 8388608
  77.5 18.9 %slice-start.1 = ((s8[8388608]{0:T(1024)(128)(4,1)}), s8[4194304]{0:T(1024)(128)(4,1)S(1)}, s32[]{:S(2)}) async-start(s8[8388608]{0:T(1024)(128)(4,1)} %bitcast.25), calls=%async_computation.8 | async-start | bytes 8388608
  77.5 18.9 %copy-start.1 = (bf16[64,64,512]{2,1,0:T(8,128)(2,1)S(1)}, bf16[64,64,512]{2,1,0:T(8,128)(2,1)}, u32[]{:S(2)}) copy-start(bf16[64,64,512]{2,1,0:T(8,128)(2,1)} %inverse_ref.3) | copy-start | bytes 12582916
  77.5 18.9 %copy-start.2 = (f32[64,1024]{1,0:T(8,128)S(1)}, f32[64,1024]{1,0:T(8,128)}, u32[]{:S(2)}) copy-start(f32[64,1024]{1,0:T(8,128)} %diagonal_ref.1) | copy-start | bytes 786436
  77.5 18.9 %copy-start.7 = (s32[2,512]{1,0:T(2,128)S(1)}, s32[2,512]{1,0:T(2,128)}, u32[]{:S(2)}) copy-start(s32[2,512]{1,0:T(2,128)} %index_ref.1) | copy-start | bytes 12292

commit v6 on v5

--- a/solution.py
+++ b/solution.py
@@ -231,11 +231,15 @@
         copies[first] = pltpu.make_async_copy(
             blocks_hbm.at[pl.ds(start + held, first + 8 - held - start)], blocks_ref.at[rows], sems.at[first // 8]
         )
-    for copy in copies.values():
-        copy.start()
+    ahead = 24
+    for first in range(0, held // 8 * 8 + ahead, 8):
+        if first in copies:
+            copies[first].start()
     for first in range(0, width, 8):
         if first in copies:
             copies[first].wait()
+            if first + ahead in copies:
+                copies[first + ahead].start()
         places = [([early_ref], a) if a < held else ([blocks_ref], a - held) for a in range(first, first + 8)]
 
         def chunk(c, _, places=places, first=first):

time: 138 us -> 138 us (level)
  no operation moved by 1% of the time
where the time goes in v6:
time: 138 us
  blocking collectives  85.1 us (62%)
  Pallas kernels  24.1 us (17%)
  starting transfers between devices  15.1 us (11%)
  waiting for transfers between devices  12.1 us (9%)
    all_to_all x5, blocking collectives, exchange(): lax.all_to_all(sent, ('stream', 'span'), split_axis=0, concat_axis=0, til...  85.1 us
    pallas_call x10, Pallas kernels, call(): pl.pallas_call(kernel, out_shape=out_shape, compiler_params=pltpu.Compile...  24.1 us
    all_to_all x2, starting transfers between devices, exchange(): lax.all_to_all(sent, ('stream', 'span'), split_axis=0, concat_axis=0, til...  15.1 us
    all_to_all x2, waiting for transfers between devices, exchange(): lax.all_to_all(sent, ('stream', 'span'), split_axis=0, concat_axis=0, til...  12.1 us
  transfers between devices with their start and end apart: 2, of which 2 were waited for; matrix products, arithmetic and copies ran while one was open for 0% of the time, Pallas kernels for 5%

profile of v6, /device:TPU:1, one launch (start us, length us, event | category | flops | bytes accessed | tf_op | source)
XLA Modules:
  0.0 138.0 jit_solution(1544198697902270704)
XLA Ops:
  0.6 0.0 copy-start
  0.6 0.0 copy-start.4
  0.7 0.0 copy-start.6
  0.7 0.0 copy-start.8
  0.7 1.9 %shard_map.131 = (s32[128,128]{1,0:T(8,128)}, s32[2,1024]{1,0:T(2,128)}) custom-call(s32[1,1024]{1,0:T(1,128)} %bitcast.43, s32[1,1024]{1,0:T(1,128)} %bitcast.44), custom_call_target="tpu_custom_call" | custom-call | flops 20000000000 | bytes 200000000 | tf_op jit(solution)/shard_map/pallas_call | solution.py:42
  2.6 11.5 %all-to-all-start = ((s32[128,1,128]{2,1,0:T(1,128)}), s32[128,1,128]{2,1,0:T(1,128)S(1)}, u32[]{:S(2)}, u32[]{:S(2)}) async-start(s32[128,1,128]{2,1,0:T(1,128)} %bitcast.42), calls=%async_computation | async-start | bytes 131072 | tf_op jit(solution)/shard_map/all_to_all | solution.py:515
  14.1 0.0 copy-done
  14.1 0.0 copy-done.4
  14.1 0.0 copy-done.6
  14.2 0.0 copy-done.8
  14.2 0.0 copy-start.5
  14.2 0.7 copy-done.5
  14.9 1.9 %shard_map.132 = (s32[2,1024]{1,0:T(2,128)S(1)}, f32[1,1024]{1,0:T(1,128)S(1)}, bf16[32,1024]{1,0:T(8,128)(2,1)S(1)}, f32[32,64]{1,0:T(8,128)S(1)}, f32[256,128]...) custom-call(s32[2,1024]{1,0:T(2,128)S(1)} %copy-done.5, ...), custom_call_target="tpu_custom_call" | custom-call | tf_op jit(solution)/shard_map/pallas_call | solution.py:42
  16.8 0.0 copy-start.3
  16.8 7.2 %all-to-all-done = s32[128,1,128]{2,1,0:T(1,128)S(1)} async-done(((s32[128,1,128]{2,1,0:T(1,128)}), s32[128,1,128]{2,1,0:T(1,128)S(1)}, u32[]{:S(2)}, u32[]{:S(2)}) %all-to-all-start) | async-done | bytes 65568 | tf_op jit(solution)/shard_map/all_to_all | solution.py:515
  23.9 0.6 shard_map.133
  24.5 17.9 %all_to_all.35 = f32[128,8,128]{2,1,0:T(8,128)S(1)} all-to-all(f32[128,8,128]{2,1,0:T(8,128)S(1)} %bitcast.32), channel_id=1, replica_groups=mesh['stream'=32,'span'=4] {'stream','span'}, dimensions={0} | all-to-all | bytes 1048576 | tf_op jit(solution)/shard_map/all_to_all | solution.py:515
  42.4 1.8 %shard_map.134 = (f32[64,1024]{1,0:T(8,128)S(1)}, f32[128,128]{1,0:T(8,128)}) custom-call(f32[1024,128]{1,0:T(8,128)S(1)} %bitcast.30, s32[2,1024]{1,0:T(2,128)S(1)} %get-tuple-element.24.ids_ref, f32[1,1024]{1,0:T(1,128)S(1)} %get-tuple-element.25.weight_ref, bf16[32,1024]{1,0:T(8,128)(2,1)S(1)} %get-tuple-element.26.chosen_ref, ...), custom_call_target="tpu_custom_call" | custom-call | tf_op jit(solution)/shard_map/pallas_call | solution.py:42
  44.3 3.6 %all-to-all-start.2 = ((f32[128,1,128]{2,1,0:T(1,128)}), f32[128,1,128]{2,1,0:T(1,128)S(1)}, u32[]{:S(2)}, u32[]{:S(2)}) async-start(f32[128,1,128]{2,1,0:T(1,128)} %bitcast.11), calls=%async_computation.2 | async-start | bytes 131072 | tf_op jit(solution)/shard_map/all_to_all | solution.py:515
  47.9 5.0 %shard_map.135.packed_ref = f32[1024,128]{1,0:T(8,128)S(1)} custom-call(bf16[14,64,1024]{2,1,0:T(8,128)(2,1)S(1)} %get-tuple-element.20.early_ref, bf16[64,64,1024]{2,1,0:T(8,128)(2,1)} %blocks_hbm.3, f32[64,1024]{1,0:T(8,128)S(1)} %get-tuple-element.28.restricted_ref, s32[2,1024]{1,0:T(2,128)S(1)} %get-tuple-element.24.ids_ref, ...), custom_call_target="tpu_custom_call" | custom-call | tf_op jit(solution)/shard_map/pallas_call | solution.py:42
  53.0 4.9 %all-to-all-done.2 = f32[128,1,128]{2,1,0:T(1,128)S(1)} async-done(((f32[128,1,128]{2,1,0:T(1,128)}), f32[128,1,128]{2,1,0:T(1,128)S(1)}, u32[]{:S(2)}, u32[]{:S(2)}) %all-to-all-start.2) | async-done | bytes 65568 | tf_op jit(solution)/shard_map/all_to_all | solution.py:515
  57.9 0.0 copy-done.3
  57.9 0.9 shard_map.136
  58.8 19.0 %all_to_all.36 = f32[128,8,128]{2,1,0:T(8,128)S(1)} all-to-all(f32[128,8,128]{2,1,0:T(8,128)S(1)} %bitcast.31), channel_id=1, replica_groups=mesh['stream'=32,'span'=4] {'stream','span'}, dimensions={0} | all-to-all | bytes 1048576 | tf_op jit(solution)/shard_map/all_to_all | solution.py:515
  77.8 1.3 shard_map.137
  79.1 17.6 %all_to_all.37 = f32[128,8,128]{2,1,0:T(8,128)S(1)} all-to-all(f32[128,8,128]{2,1,0:T(8,128)S(1)} %bitcast.34), channel_id=1, replica_groups=mesh['stream'=32,'span'=4] {'stream','span'}, dimensions={0} | all-to-all | bytes 1048576 | tf_op jit(solution)/shard_map/all_to_all | solution.py:515
  96.7 0.0 slice-done
  96.7 8.1 %shard_map.138 = f32[1024,128]{1,0:T(8,128)S(1)} custom-call(f32[1024,128]{1,0:T(8,128)S(1)} %bitcast.27, s32[2,1024]{1,0:T(2,128)S(1)} %get-tuple-element.24.ids_ref, s32[2,512]{1,0:T(2,128)S(1)} %copy-done.7, f32[64,1024]{1,0:T(8,128)S(1)} %copy-done.2, bf16[2,64,64,512]{3,2,1,0:T(8,128)(2,1)S(1)} %bitcast.26, bf16[64,64,512]{2,1,0:T(8,128)(2,1)S(1)} %copy-done.1), custom_call_target="tpu_custom_call" | custom-call | tf_op jit(solution)/shard_map/pallas_call | solution.py:42
  104.9 17.5 %all_to_all.38 = f32[128,8,128]{2,1,0:T(8,128)S(1)} all-to-all(f32[128,8,128]{2,1,0:T(8,128)S(1)} %bitcast.28), channel_id=1, replica_groups=mesh['stream'=32,'span'=4] {'stream','span'}, dimensions={0} | all-to-all | bytes 1048576 | tf_op jit(solution)/shard_map/all_to_all | solution.py:515
  122.3 1.1 shard_map.139
  123.5 13.2 %all_to_all.39 = f32[128,1,128]{2,1,0:T(1,128)S(1)} all-to-all(f32[128,1,128]{2,1,0:T(1,128)S(1)} %bitcast.38), channel_id=1, replica_groups=mesh['stream'=32,'span'=4] {'stream','span'}, dimensions={0} | all-to-all | bytes 131072 | tf_op jit(solution)/shard_map/all_to_all | solution.py:515
  136.7 1.3 shard_map.140
  (10 shorter events, 0.0 us)
Async XLA Ops:
  0.6 13.5 %copy-start = (f32[4,64,512]{2,1,0:T(8,128)S(1)}, f32[4,64,512]{2,1,0:T(8,128)}, u32[]{:S(2)}) copy-start(f32[4,64,512]{2,1,0:T(8,128)} %basis_ref.5) | copy-start | bytes 1572868
  0.6 13.5 %copy-start.4 = (f32[64,32]{0,1:T(8,128)S(1)}, f32[64,32]{0,1:T(8,128)}, u32[]{:S(2)}) copy-start(f32[64,32]{0,1:T(8,128)} %param.18) | copy-start | bytes 24580
  0.7 13.5 %copy-start.6 = (f32[1024]{0:T(1024)S(1)}, f32[1024]{0:T(1024)}, u32[]{:S(2)}) copy-start(f32[1024]{0:T(1024)} %param.15) | copy-start | bytes 12292
  0.7 13.5 %copy-start.8 = (s32[32]{0:T(128)S(1)}, s32[32]{0:T(128)}, u32[]{:S(2)}) copy-start(s32[32]{0:T(128)} %param.17) | copy-start | bytes 388
  2.6 21.3 %all-to-all-start = ((s32[128,1,128]{2,1,0:T(1,128)}), s32[128,1,128]{2,1,0:T(1,128)S(1)}, u32[]{:S(2)}, u32[]{:S(2)}) async-start(s32[128,1,128]{2,1,0:T(1,128)} %bitcast.42), calls=%async_computation | async-start | bytes 131072 | tf_op jit(solution)/shard_map/all_to_all | solution.py:515
  14.2 0.7 copy-start.5
  16.8 41.1 %copy-start.3 = (f32[32,1024]{1,0:T(8,128)S(1)}, f32[32,1024]{1,0:T(8,128)}, u32[]{:S(2)}) copy-start(f32[32,1024]{1,0:T(8,128)} %inverse_ref.2) | copy-start | bytes 393220
  44.3 13.6 %all-to-all-start.2 = ((f32[128,1,128]{2,1,0:T(1,128)}), f32[128,1,128]{2,1,0:T(1,128)S(1)}, u32[]{:S(2)}, u32[]{:S(2)}) async-start(f32[128,1,128]{2,1,0:T(1,128)} %bitcast.11), calls=%async_computation.2 | async-start | bytes 131072 | tf_op jit(solution)/shard_map/all_to_all | solution.py:515
  57.9 38.8 %slice-start = ((s8[8388608]{0:T(1024)(128)(4,1)}), s8[4194304]{0:T(1024)(128)(4,1)S(1)}, s32[]{:S(2)}) async-start(s8[8388608]{0:T(1024)(128)(4,1)} %bitcast.25), calls=%async_computation.7 | async-start | bytes 8388608
  77.7 18.9 %slice-start.1 = ((s8[8388608]{0:T(1024)(128)(4,1)}), s8[4194304]{0:T(1024)(128)(4,1)S(1)}, s32[]{:S(2)}) async-start(s8[8388608]{0:T(1024)(128)(4,1)} %bitcast.25), calls=%async_computation.8 | async-start | bytes 8388608
  77.7 18.9 %copy-start.1 = (bf16[64,64,512]{2,1,0:T(8,128)(2,1)S(1)}, bf16[64,64,512]{2,1,0:T(8,128)(2,1)}, u32[]{:S(2)}) copy-start(bf16[64,64,512]{2,1,0:T(8,128)(2,1)} %inverse_ref.3) | copy-start | bytes 12582916
  77.7 18.9 %copy-start.2 = (f32[64,1024]{1,0:T(8,128)S(1)}, f32[64,1024]{1,0:T(8,128)}, u32[]{:S(2)}) copy-start(f32[64,1024]{1,0:T(8,128)} %diagonal_ref.1) | copy-start | bytes 786436
  77.8 18.9 %copy-start.7 = (s32[2,512]{1,0:T(2,128)S(1)}, s32[2,512]{1,0:T(2,128)}, u32[]{:S(2)}) copy-start(s32[2,512]{1,0:T(2,128)} %index_ref.1) | copy-start | bytes 12292
